TPU v7x, 32 devices: a whole 2x2x4 slice. The times are simulated.
32 devices in a mesh: dp: 8 (over y, x, core), mp: 4 (over z).
Axes of the slice: x: 2, y: 2, z: 4, core: 2. Of those that a mesh axis runs over, the one named last changes fastest.
Arguments:
- block_input: float32 [16384, 1024], P(('dp', 'mp')), may hold values from -6 to 6
- lengths: int32 [8], P('dp'), may hold values from 1537 to 2048, as said below
- mixer_gain: float32 [1024], replicated, may hold values from 0.5 to 1.5
- mixer_shift: float32 [1024], replicated, may hold values from -1.25 to 1.25
- input_weight: bfloat16 [1024, 3, 1024], P(None, None, 'mp'), may hold values from -0.1875 to 0.1875
- input_bias: float32 [3, 1024], P(None, 'mp'), may hold values from -1.25 to 1.25
- conv_weight: float32 [3, 3, 1024], P(None, None, 'mp'), may hold values from -3.5 to 3.5
- conv_bias: float32 [3, 1024], P(None, 'mp'), may hold values from -1.25 to 1.25
- enter_weight: float32 [33, 64], replicated, may hold values from -3.5 to 3.5
- enter_bias: float32 [64], replicated, may hold values from -3.140625 to 3.140625
- middle_weight: float32 [64, 64], replicated, may hold values from -1.5 to 1.5
- middle_bias: float32 [64], replicated, may hold values from -3.140625 to 3.140625
- inner_weight: float32 [64, 64], replicated, may hold values from -1.5 to 1.5
- inner_bias: float32 [64], replicated, may hold values from -3.140625 to 3.140625
- frequency: float32 [64], replicated, may hold values from 0.5 to 1.5
- filter_weight: float32 [64, 1024], P(None, 'mp'), may hold values from -0.015625 to 0.015625
- skip_scale: float32 [1024], P('mp'), may hold values from -6 to 6
- output_weight: bfloat16 [1024, 1024], P('mp'), may hold values from -0.1875 to 0.1875
- output_bias: float32 [1024], replicated, may hold values from -1.25 to 1.25
- feed_gain: float32 [1024], replicated, may hold values from 0.5 to 1.5
- feed_shift: float32 [1024], replicated, may hold values from -1.25 to 1.25
- expand_weight: bfloat16 [1024, 4096], P(None, 'mp'), may hold values from -0.1875 to 0.1875
- expand_bias: float32 [4096], P('mp'), may hold values from -1.25 to 1.25
- reduce_weight: bfloat16 [4096, 1024], P('mp'), may hold values from -0.09375 to 0.09375
- reduce_bias: float32 [1024], replicated, may hold values from -1.25 to 1.25
- cotangent: float32 [16384, 1024], P(('dp', 'mp')), may hold values from -6 to 6
Outputs:
- result: float32 [16384, 1024], P(('dp', 'mp'))
- input_grad: float32 [16384, 1024], P(('dp', 'mp'))
- mixer_gain_grad: float32 [1024], replicated
- mixer_shift_grad: float32 [1024], replicated
- input_weight_grad: float32 [1024, 3, 1024], P(None, None, 'mp')
- input_bias_grad: float32 [3, 1024], P(None, 'mp')
- conv_weight_grad: float32 [3, 3, 1024], P(None, None, 'mp')
- conv_bias_grad: float32 [3, 1024], P(None, 'mp')
- enter_weight_grad: float32 [33, 64], replicated
- enter_bias_grad: float32 [64], replicated
- middle_weight_grad: float32 [64, 64], replicated
- middle_bias_grad: float32 [64], replicated
- inner_weight_grad: float32 [64, 64], replicated
- inner_bias_grad: float32 [64], replicated
- frequency_grad: float32 [64], replicated
- filter_weight_grad: float32 [64, 1024], P(None, 'mp')
- skip_scale_grad: float32 [1024], P('mp')
- output_weight_grad: float32 [1024, 1024], P('mp')
- output_bias_grad: float32 [1024], replicated
- feed_gain_grad: float32 [1024], replicated
- feed_shift_grad: float32 [1024], replicated
- expand_weight_grad: float32 [1024, 4096], P(None, 'mp')
- expand_bias_grad: float32 [4096], P('mp')
- reduce_weight_grad: float32 [4096, 1024], P('mp')
- reduce_bias_grad: float32 [1024], replicated
Inputs may be any that keep to these rules, and one draw needn't show every extreme that they name: `lengths`: each sequence uses more than three quarters of its 2048 slots; in every draw some sequence uses all of them.
All inputs are finite; a program needn't handle non-finite values.
Results may differ from a plain program's by a relative error of at most 0.017.
Values may be sent and summed in bfloat16 or wider, within the bound.
No kernel may reach another device: no remote copies, remote signals or barrier semaphores. Data moves between devices by JAX's collectives and lax.ppermute only.
A program may use at most 192 MiB of HBM per device.

v0:
```python
import functools
import math

import jax
import jax.numpy as jnp
import ml_dtypes
import numpy as np
from jax import lax
from jax.experimental import pallas as pl
from jax.experimental.pallas import tpu as pltpu
from jax.sharding import PartitionSpec as P

HIGHEST_MODE = lax.Precision.HIGHEST
EPSILON = 1e-05
FIRST_FACTOR = 64
CHUNK = 16
F32 = jnp.float32
BF16 = jnp.bfloat16
VMEM_SPEC = pl.BlockSpec(memory_space=pltpu.VMEM)
SMEM_SPEC = pl.BlockSpec(memory_space=pltpu.SMEM)
ANY_SPEC = pl.BlockSpec(memory_space=pl.ANY)
HBM_SPEC = pl.BlockSpec(memory_space=pltpu.HBM)


def norm_parts(values_in):
    centred = values_in - jnp.mean(values_in, axis=-1, keepdims=True)
    variance = jnp.mean(centred * centred, axis=-1, keepdims=True)
    scale = lax.rsqrt(variance + EPSILON)
    return centred * scale, scale


def norm_back(normal, scale, gain, grad):
    inner = grad * gain
    part = scale * (
        inner
        - jnp.mean(inner, axis=-1, keepdims=True)
        - normal * jnp.mean(inner * normal, axis=-1, keepdims=True)
    )
    return part, jnp.sum(grad * normal, axis=0), jnp.sum(grad, axis=0)


FEATURE_ROWS = 40
TAP_STEP = 256


def position_features(total, emb_count):
    place = np.arange(total, dtype=np.float64)
    bands = (emb_count - 1) // 2
    freq_grid = 1e-4 + np.arange(bands) * ((bands - 1 - 1e-4) / (bands - 1))
    angles = 2.0 * math.pi / total * freq_grid[:, None] * place[None, :]
    rows = np.concatenate([place[None] / (total - 1), np.cos(angles), -np.sin(angles)])
    rows = np.pad(rows, ((0, FEATURE_ROWS - emb_count), (0, 0)))
    return jnp.asarray(rows.astype(np.float32))


def exact(left, right, left_dim, right_dim):
    dims = (((left_dim,), (right_dim,)), ((), ()))
    return lax.dot_general(
        left, right, dims, precision=HIGHEST_MODE, preferred_element_type=F32
    )


def decay_block(first_row, rows, channels, seq_len, channel_total, group):
    slowest = math.log(0.01) / 1.5
    fastest = math.log(0.01) / 0.3
    row = lax.broadcasted_iota(jnp.int32, (rows, channels), 0) + first_row
    channel = lax.broadcasted_iota(jnp.int32, (rows, channels), 1) + group * channels
    rates = jnp.abs(slowest + (fastest - slowest) * channel.astype(F32) / (channel_total - 1))
    return jnp.exp(-(row.astype(F32) / (seq_len - 1)) * rates)


def filter_kernel(
    channel_total, here_ref, features_ref, enter_ref, middle_ref, inner_ref, columns_ref, filter_ref, *outs
):
    taps_ref, value_ref, sine_ref, cosine_ref = outs
    seq_len, channels = taps_ref.shape
    frequency = columns_ref[:, 3:4]
    hidden = features_ref[...]
    for n, weight_ref in enumerate((enter_ref, middle_ref, inner_ref)):
        value = exact(weight_ref[...], hidden, 0, 0) + columns_ref[:, n : n + 1]
        value_ref[n] = value
        hidden = jnp.sin(frequency * value)
        sine_ref[n] = hidden
        cosine_ref[n] = jnp.cos(frequency * value)
    for start in range(0, seq_len, TAP_STEP):
        rows = slice(start, start + TAP_STEP)
        decay = decay_block(start, TAP_STEP, channels, seq_len, channel_total, here_ref[1])
        taps = exact(sine_ref[2, :, rows], filter_ref[...], 0, 0)
        taps_ref[rows, :] = (taps * decay).astype(BF16)


def filter_back_kernel(
    channel_total,
    here_ref,
    features_ref,
    middle_ref,
    inner_ref,
    columns_ref,
    filter_ref,
    value_ref,
    sine_ref,
    cosine_ref,
    grad_ref,
    packed_ref,
    filter_grad_ref,
    hidden_ref,
):
    seq_len, channels = grad_ref.shape
    units = filter_ref.shape[0]
    frequency = columns_ref[:, 3:4]
    filter_grad_ref[...] = jnp.zeros_like(filter_grad_ref)
    for start in range(0, seq_len, TAP_STEP):
        rows = slice(start, start + TAP_STEP)
        decay = decay_block(start, TAP_STEP, channels, seq_len, channel_total, here_ref[1])
        grad = grad_ref[rows, :] * decay
        filter_grad_ref[...] += exact(sine_ref[2, :, rows], grad, 1, 0)
        hidden_ref[:, rows] = exact(filter_ref[...], grad, 1, 1)
    packed_ref[...] = jnp.zeros_like(packed_ref)
    grad = hidden_ref[...]
    frequency_grad = jnp.zeros((units, 1), F32)
    for n in (2, 1, 0):
        inside = grad * cosine_ref[n]
        frequency_grad += jnp.sum(inside * value_ref[n], axis=1, keepdims=True)
        inside = inside * frequency
        packed_ref[:, 3 * units + n : 3 * units + n + 1] = jnp.sum(inside, axis=1, keepdims=True)
        below = features_ref[...] if n == 0 else sine_ref[n - 1]
        packed_ref[: below.shape[0], n * units : (n + 1) * units] = exact(below, inside, 1, 1)
        if n > 0:
            grad = exact((middle_ref, inner_ref)[n - 1][...], inside, 1, 0)
    packed_ref[:, 3 * units + 3 : 3 * units + 4] = frequency_grad


def spectral_tables(seq_len):
    total = 2 * seq_len
    count1 = FIRST_FACTOR
    count2 = total // count1
    half = count1 // 2
    slot = np.arange(half)
    t1 = np.arange(half)
    t2 = np.arange(count2)
    k2 = np.arange(count2)
    angle = 2 * np.pi * slot[:, None] * t1[None, :] / count1
    first = np.zeros((half, 2, half))
    first[:, 0] = np.cos(angle)
    first[:, 1] = -np.sin(angle)
    first[0, 1] = (-1.0) ** t1
    last = np.zeros((half, half, 2))
    last[:, :, 0] = np.cos(angle.T) / seq_len
    last[:, :, 1] = -np.sin(angle.T) / seq_len
    last[:, 0, 0] = 1.0 / total
    last[:, 0, 1] = (-1.0) ** t1 / total
    mid = np.zeros((half, 2, count2, 2, count2))
    back = np.zeros((half, 2, count2, 2, count2))
    for s in range(1, half):
        turn = np.exp(-2j * np.pi * t2[None, :] * (s / total + k2[:, None] / count2))
        mid[s, 0, :, 0] = turn.real
        mid[s, 0, :, 1] = -turn.imag
        mid[s, 1, :, 0] = turn.imag
        mid[s, 1, :, 1] = turn.real
        undo = np.conj(turn).T
        back[s, 0, :, 0] = undo.real
        back[s, 0, :, 1] = -undo.imag
        back[s, 1, :, 0] = undo.imag
        back[s, 1, :, 1] = undo.real
    h2 = count2 // 2
    turn = np.exp(-2j * np.pi * t2[None, :] * k2[:h2, None] / count2)
    mid[0, 0, :h2, 0] = turn.real
    mid[0, 1, :h2, 0] = turn.imag
    mid[0, 1, 0, 0] = (-1.0) ** t2
    back[0, 0, :, 0, :h2] = 2 * turn.real.T
    back[0, 0, :, 1, :h2] = 2 * turn.imag.T
    back[0, 0, :, 0, 0] = 1.0
    back[0, 0, :, 1, 0] = (-1.0) ** t2
    turn = np.exp(-2j * np.pi * t2[None, :] * (half / total + k2[:h2, None] / count2))
    mid[0, 0, h2:, 1] = turn.real
    mid[0, 1, h2:, 1] = turn.imag
    back[0, 1, :, 0, h2:] = 2 * turn.real.T
    back[0, 1, :, 1, h2:] = 2 * turn.imag.T
    unit = np.eye(CHUNK)
    tables = (
        np.kron(first.reshape(count1, half), unit),
        mid.reshape(half, 2 * count2, 2 * count2),
        back.reshape(half, 2 * count2, 2 * count2),
        np.kron(last.reshape(half, count1), unit),
    )
    return tuple(jnp.asarray(v.astype(np.float32).astype(ml_dtypes.bfloat16)) for v in tables)


def times(left, right):
    return jnp.dot(left, right, preferred_element_type=F32)


def stage_first(first_ref, x_ref, y_ref):
    count1, count2, cols = y_ref.shape
    for j in range(count2 // CHUNK):
        rows = slice(CHUNK * j, CHUNK * (j + 1))
        block = x_ref[:, rows, :].reshape(count1 // 2 * CHUNK, cols)
        y_ref[:, rows, :] = times(first_ref[...], block).reshape(count1, CHUNK, cols).astype(BF16)


def stage_last(last_ref, z_ref, out_ref):
    count1, count2, cols = z_ref.shape
    for j in range(count2 // CHUNK):
        rows = slice(CHUNK * j, CHUNK * (j + 1))
        block = z_ref[:, rows, :].reshape(count1 * CHUNK, cols)
        values = times(last_ref[...], block).reshape(count1 // 2, CHUNK, cols)
        out_ref[:, rows, :] = values.astype(out_ref.dtype)


def spectral_product(s, left_re, left_im, right_re, right_im, sign):
    both_re = left_re * right_re
    both_im = left_im * right_im
    row = lax.broadcasted_iota(jnp.int32, both_re.shape, 0)
    real_row = (row == 0) & (s == 0)
    out_re = jnp.where(real_row, both_re, both_re - sign * both_im)
    out_im = jnp.where(real_row, both_im, left_im * right_re + sign * left_re * right_im)
    return jnp.concatenate([out_re, out_im], axis=0).astype(BF16)


def conv_kernel(
    first_ref, mid_ref, back_ref, last_ref, u_ref, t_ref, out_ref, su_out, st_out, *refs
):
    y_ref, z_ref, su_ref, st_ref, sems = refs
    count1, count2, cols = y_ref.shape
    stage_first(first_ref, u_ref, y_ref)
    stage_first(first_ref, t_ref, z_ref)

    def slot_step(s, carry):
        pair = pl.ds(2 * s, 2)
        spec_u = times(mid_ref[s], y_ref[pair].reshape(2 * count2, cols))
        spec_t = times(mid_ref[s], z_ref[pair].reshape(2 * count2, cols))
        su_ref[pair] = spec_u.astype(BF16).reshape(2, count2, cols)
        st_ref[pair] = spec_t.astype(BF16).reshape(2, count2, cols)
        product = spectral_product(
            s, spec_u[:count2], spec_u[count2:], spec_t[:count2], spec_t[count2:], 1
        )
        z_ref[pair] = times(back_ref[s], product).astype(BF16).reshape(2, count2, cols)
        return carry

    lax.fori_loop(0, count1 // 2, slot_step, 0, unroll=2)
    stores = [
        pltpu.make_async_copy(su_ref, su_out, sems.at[0]),
        pltpu.make_async_copy(st_ref, st_out, sems.at[1]),
    ]
    for copy in stores:
        copy.start()
    stage_last(last_ref, z_ref, out_ref)
    for copy in stores:
        copy.wait()


def conv_back_kernel(
    first_ref, mid_ref, back_ref, last_ref, g_ref, su_any, st_any, *refs
):
    du_ref, dt_ref, y_ref, z_ref, x_ref, su_ref, st_ref, sems = refs
    count1, count2, cols = y_ref.shape
    loads = [
        pltpu.make_async_copy(su_any, su_ref, sems.at[0]),
        pltpu.make_async_copy(st_any, st_ref, sems.at[1]),
    ]
    for copy in loads:
        copy.start()
    stage_first(first_ref, g_ref, y_ref)

    for copy in loads:
        copy.wait()

    def slot_step(s, carry):
        pair = pl.ds(2 * s, 2)
        spec_g = times(mid_ref[s], y_ref[pair].reshape(2 * count2, cols))
        spec_u = su_ref[pair].astype(F32)
        spec_t = st_ref[pair].astype(F32)
        product = spectral_product(s, spec_g[:count2], spec_g[count2:], spec_t[0], spec_t[1], -1)
        y_ref[pair] = times(back_ref[s], product).astype(BF16).reshape(2, count2, cols)
        product = spectral_product(s, spec_g[:count2], spec_g[count2:], spec_u[0], spec_u[1], -1)
        z_ref[pair] = times(back_ref[s], product).astype(BF16).reshape(2, count2, cols)
        return carry

    lax.fori_loop(0, count1 // 2, slot_step, 0, unroll=2)
    stage_last(last_ref, y_ref, x_ref)
    stage_last(last_ref, z_ref, dt_ref)
    groups, rows, _ = du_ref.shape
    rows -= CHUNK
    step = count1 // 2 // groups
    for place in range(groups):
        block = x_ref[place * step : (place + 1) * step]
        du_ref[place, :rows, :] = block.reshape(rows, cols)
        du_ref[place, rows:, :] = x_ref[(place + 1) % groups * step, :CHUNK, :]


def kernel_call(kernel, name, outs, in_specs, scratch, flops, size, limit, args, copied=()):
    return pl.pallas_call(
        kernel,
        out_shape=tuple(jax.ShapeDtypeStruct(shape, dtype) for shape, dtype in outs),
        in_specs=in_specs,
        out_specs=tuple(HBM_SPEC if n in copied else VMEM_SPEC for n in range(len(outs))),
        scratch_shapes=scratch,
        compiler_params=pltpu.CompilerParams(vmem_limit_bytes=limit << 20),
        cost_estimate=pl.CostEstimate(flops=flops, bytes_accessed=size << 20, transcendentals=0),
        name=name,
    )(*args)


def long_conv(tables, signal, taps):
    seq_len, cols = taps.shape
    count1 = FIRST_FACTOR
    count2 = 2 * seq_len // count1
    timed = (count1 // 2, count2, cols)
    spectral = (count1, count2, cols)
    out, spec_u, spec_t = kernel_call(
        conv_kernel,
        "long_conv",
        [(timed, BF16), (spectral, BF16), (spectral, BF16)],
        [VMEM_SPEC] * 6,
        [pltpu.VMEM(spectral, BF16)] * 4 + [pltpu.SemaphoreType.DMA((2,))],
        9_000_000_000,
        14,
        40,
        (*tables, signal.reshape(timed), taps.reshape(timed)),
        copied=(1, 2),
    )
    return out.reshape(signal.shape), spec_u, spec_t


def long_conv_back(tables, grad, spec_u, spec_t):
    groups, rows, cols = grad.shape
    count1 = FIRST_FACTOR
    count2 = 2 * groups * rows // count1
    timed = (count1 // 2, count2, cols)
    spectral = (count1, count2, cols)
    grad_u, grad_t = kernel_call(
        conv_back_kernel,
        "long_conv_back",
        [((groups, rows + CHUNK, cols), BF16), (timed, F32)],
        [VMEM_SPEC] * 5 + [HBM_SPEC] * 2,
        [pltpu.VMEM(spectral, BF16)] * 2
        + [pltpu.VMEM(timed, BF16)]
        + [pltpu.VMEM(spectral, BF16)] * 2
        + [pltpu.SemaphoreType.DMA((2,))],
        9_000_000_000,
        14,
        40,
        (*tables, grad.reshape(timed), spec_u, spec_t),
    )
    return grad_u, grad_t.reshape(groups * rows, cols)


def shift_mp(values_in, count):
    size = lax.axis_size("mp")
    return lax.ppermute(values_in, "mp", [(i, (i + count) % size) for i in range(size)])


def swap_dp(values_in, bit):
    size = lax.axis_size("dp")
    return lax.ppermute(values_in, "dp", [(i, i ^ (1 << bit)) for i in range(size)])


def bit_orders():
    bits = lax.axis_size("dp").bit_length() - 1
    high = list(range(1, bits))
    return [0] + high, [0] + high[::-1]


def after(values_in, *others):
    return lax.optimization_barrier((values_in,) + others)[0]


def gather_offsets(half):
    first, second = ((4, 2), (2, 4))[half]
    return [(0, first), (second, first | second), (1, first | 1), (second | 1, first | second | 1)]


def gather_start(block, half, *beside):
    bit = bit_orders()[half][2]
    return jnp.stack([after(block, *beside) if beside else block, swap_dp(block, bit)])


def gather_rest(pair, half, *beside):
    others = swap_dp(pair, bit_orders()[half][1])
    if beside:
        others = after(others, *beside)
    return [pair, others, swap_dp(pair, 0), swap_dp(others, 0)]


def split_blocks(pieces, axis, rows, *beside):
    out = []
    for half in range(2):
        part = lax.slice_in_dim(pieces, half * rows, (half + 1) * rows, axis=axis)
        out.extend(gather_rest(gather_start(part, half), half, *beside))
    return out


def add_across(part, bit, *beside):
    keep = after(part[0], *beside) if beside else part[0]
    return (keep.astype(F32) + swap_dp(part[1], bit).astype(F32)).astype(BF16)


def sum_groups(mine):
    total = mine[0].astype(F32)
    for k in range(1, lax.axis_size("mp")):
        total = total + shift_mp(mine[k], -k).astype(F32)
    return total


def own_group(grads):
    return lax.psum(sum_groups(grads), "dp")


def each_block(here, blocks):
    for half in range(2):
        for n, offsets in enumerate(gather_offsets(half)):
            for i, offset in enumerate(offsets):
                yield blocks[4 * half + n].at[i], half, here ^ offset


def place_feed_kernel(here_ref, *refs):
    *blocks, expand_ref, reduce_ref = refs
    share = blocks[0].shape[1]
    for block, half, index in each_block(here_ref[0], blocks):
        place = pl.ds(pl.multiple_of(index * share, share), share)
        if half == 0:
            expand_ref[:, place] = block[...].astype(F32).T
        else:
            reduce_ref[place, :] = block[...].astype(F32)


def place_input_kernel(here_ref, *refs):
    *blocks, input_ref, output_ref, full_ref = refs
    rows = blocks[0].shape[2]
    parts = full_ref.shape[0]
    for block, half, index in each_block(here_ref[0], blocks):
        place = pl.ds(pl.multiple_of((index * 2 + half) * rows, rows), rows)
        full_ref[:, place, :] = block[:parts].astype(F32)
        output_ref[place, :] = block[parts].astype(F32)
    for p in range(parts):
        input_ref[p] = full_ref[p].T


def sum_dp(values_in):
    for bit in range(lax.axis_size("dp").bit_length() - 1):
        values_in = values_in + swap_dp(values_in, bit)
    return values_in


def contract_rows(left, right):
    return lax.dot_general(left, right, (((0,), (0,)), ((), ())), preferred_element_type=F32)


def contract_cols(left, right):
    return lax.dot_general(left, right, (((1,), (1,)), ((), ())), preferred_element_type=F32)


def gelu_parts(value):
    factor = math.sqrt(2.0 / math.pi)
    square = value * value
    tanh_part = jnp.tanh(factor * value * (1.0 + 0.044715 * square))
    half = 0.5 * (1.0 + tanh_part)
    slope = half + 0.5 * value * (1.0 - tanh_part * tanh_part) * (
        factor * (1.0 + 3.0 * 0.044715 * square)
    )
    return value * half, slope


ROW_STEP = 32
SMALL_ROWS = 32


def fold_rows(wide_ref, narrow_ref):
    channels = narrow_ref.shape[1]
    for i in range(wide_ref.shape[1] // channels):
        narrow_ref[8 * i : 8 * i + 8, :] = wide_ref[:, i * channels : (i + 1) * channels]


def unfold_rows(narrow):
    rows, channels = narrow.shape
    return narrow.reshape(rows // 8, 8, channels).transpose(1, 0, 2).reshape(8, -1)


def store_grad(refs, k, part, here, values):
    rows = values.shape[0] // 8
    for i in range(4):
        bit1, bit2 = (i & 1) ^ (here >> 1 & 1), (i >> 1) ^ (here >> 2)
        first, second = (bit2, bit1) if k < 2 else (bit1, bit2)
        pair = [values[(2 * i + n) * rows : (2 * i + n + 1) * rows].astype(BF16) for n in range(2)]
        even = here & 1 == 0
        refs[0][k // 2, first, second, part] = jnp.where(even, pair[0], pair[1])
        refs[1][k // 2, first, second, part] = jnp.where(even, pair[1], pair[0])


def start_input_weights(here_ref, local, blocks, weight_ref, sem):
    others = pl.ds(1, weight_ref.shape[0] - 1)
    pltpu.make_async_copy(local, weight_ref.at[0], sem).start()
    if len(blocks) == 1:
        pltpu.make_async_copy(blocks[0], weight_ref.at[others], sem).start()
        return
    rows = blocks[0].shape[3]
    for block, half, index in each_block(here_ref[0], blocks):
        start = pl.multiple_of((index * 2 + half) * rows, rows)
        pltpu.make_async_copy(block, weight_ref.at[others, :, pl.ds(start, rows)], sem).start()


def group_at(here_ref, k, groups):
    return lax.rem(here_ref[1] + (groups - k), groups)


def wait_whole(ref, sem):
    pltpu.make_async_copy(ref, ref, sem).wait()


def enter_kernel(count, here_ref, input_ref, halo_ref, vectors_ref, small_ref, local_ref, *refs):
    blocks = refs[:count]
    outs = refs[count : count + 5]
    weight_ref, rows_ref, sem, *results, out_sems = refs[count + 5 :]
    conv_input_ref, second_ref, gates_ref, projected_ref, normed_ref = results

    def store(n, k):
        return pltpu.make_async_copy(results[n].at[k], outs[n].at[k], out_sems.at[n, k])

    store_normed = pltpu.make_async_copy(normed_ref, outs[4], out_sems.at[4, 0])
    rows = input_ref.shape[0]
    groups, _, channels = conv_input_ref.shape
    start_input_weights(here_ref, local_ref, blocks, weight_ref, sem)

    def normed(values):
        return (norm_parts(values)[0] * vectors_ref[0:1] + vectors_ref[1:2]).astype(BF16)

    rows_ref[:CHUNK, :] = normed(halo_ref[...])

    def norm_step(i, carry):
        start = pl.multiple_of(i * ROW_STEP, ROW_STEP)
        values = normed(input_ref[pl.ds(start, ROW_STEP), :])
        normed_ref[pl.ds(start, ROW_STEP), :] = values
        rows_ref[pl.ds(start + CHUNK, ROW_STEP), :] = values
        return carry

    lax.fori_loop(0, rows // ROW_STEP, norm_step, 0)
    store_normed.start()
    wait_whole(weight_ref, sem)
    row = lax.broadcasted_iota(jnp.int32, (rows + CHUNK, channels), 0)
    begins = (row < CHUNK) & (here_ref[1] == 0)
    for k in range(groups):
        mixed = []
        for p in range(3):
            small = small_ref[k, 8 * p : 8 * p + 8, :]
            values = contract_cols(rows_ref[...], weight_ref[k, p]) + small[0:1]
            values = jnp.where(begins, 0.0, values)
            projected_ref[k, p] = values.astype(BF16)
            mixed.append(
                small[1:2] * values[CHUNK:]
                + small[2:3] * values[CHUNK - 1 : -1]
                + small[3:4] * values[CHUNK - 2 : -2]
                + small[4:5]
            )
        group = group_at(here_ref, k, groups)
        conv_input_ref[group] = (mixed[1] * mixed[0]).astype(BF16)
        gates_ref[k, 0] = mixed[0].astype(BF16)
        gates_ref[k, 1] = mixed[1].astype(BF16)
        second_ref[k] = mixed[2].astype(BF16)
        for n in range(4):
            store(n, group if n == 0 else k).start()
    store_normed.wait()
    for k in range(groups):
        for n in range(4):
            store(n, k).wait()


def enter(here, block_input, halo, vectors, small, local, blocks):
    rows, width = block_input.shape
    parts, channels, _ = local.shape
    groups = small.shape[0]
    outs = [
        ((groups, rows, channels), BF16),
        ((groups, rows, channels), BF16),
        ((groups, 2, rows, channels), BF16),
        ((groups, parts, rows + CHUNK, channels), BF16),
        ((rows, width), BF16),
    ]
    return kernel_call(
        functools.partial(enter_kernel, len(blocks)),
        "enter",
        outs,
        [SMEM_SPEC] + [VMEM_SPEC] * 4 + [ANY_SPEC] * (1 + len(blocks)),
        [
            pltpu.VMEM((groups, parts, channels, width), BF16),
            pltpu.VMEM((rows + CHUNK, width), BF16),
            pltpu.SemaphoreType.DMA,
            *[pltpu.VMEM(shape, dtype) for shape, dtype in outs],
            pltpu.SemaphoreType.DMA((5, groups)),
        ],
        2 * rows * width * parts * groups * channels,
        16,
        40,
        (here, block_input, halo, vectors, small, local, *blocks),
        copied=(0, 1, 2, 3, 4),
    )


def middle_kernel(count, sorted_units, here_ref, *refs):
    long_ref, conv_ref, second_ref, input_ref, cot_ref, vectors_ref, small_ref, bias_ref = refs[:8]
    expand_local, reduce_local, output_local = refs[8:11]
    blocks = refs[11 : 11 + count]
    (
        result_ref,
        hidden_grad_ref,
        conv_grad_ref,
        second_grad_ref,
        gated_ref,
        act_ref,
        pre_grad_ref,
        normed_ref,
        mix_ref,
        out_low_ref,
        bias_grad_ref,
        all_sums_ref,
        skip_grad_ref,
    ) = refs[11 + count : 24 + count]
    expand_ref, reduce_ref, output_ref, normal_ref, scale_ref, sums_ref, sems = refs[
        24 + count : 31 + count
    ]
    early_outs = (act_ref, pre_grad_ref, normed_ref, out_low_ref)
    act_ref, pre_grad_ref, normed_ref, out_low_ref, out_sems = refs[31 + count :]
    stores = [
        pltpu.make_async_copy(source, target, out_sems.at[n])
        for n, (source, target) in enumerate(
            zip((act_ref, pre_grad_ref, normed_ref, out_low_ref), early_outs)
        )
    ]
    rows, width = input_ref.shape
    groups, hidden, _ = expand_ref.shape
    channels = output_ref.shape[1]
    others = pl.ds(1, groups - 1)
    here = here_ref[0]

    pltpu.make_async_copy(output_local, output_ref.at[0], sems.at[0]).start()
    pltpu.make_async_copy(expand_local, expand_ref.at[0], sems.at[1]).start()
    pltpu.make_async_copy(reduce_local, reduce_ref.at[0], sems.at[2]).start()
    if sorted_units:
        share = hidden // 8
        half_share = channels // 16
        for block, half, index in each_block(here, blocks):
            ref = (expand_ref, reduce_ref)[half]
            start = pl.multiple_of((index * 2 + half) * half_share, half_share)
            pltpu.make_async_copy(
                block.at[:, pl.ds(share, half_share)],
                output_ref.at[others, pl.ds(start, half_share)],
                sems.at[0],
            ).start()
            start = pl.multiple_of(index * share, share)
            pltpu.make_async_copy(
                block.at[:, pl.ds(0, share)],
                ref.at[others, pl.ds(start, share)],
                sems.at[1 + half],
            ).start()
    else:
        for n, (block, ref) in enumerate(zip(blocks, (output_ref, expand_ref, reduce_ref))):
            pltpu.make_async_copy(block, ref.at[others], sems.at[n]).start()

    position = here_ref[1] * rows + lax.broadcasted_iota(jnp.int32, (rows, channels), 0)
    mask = jnp.where(position < here_ref[2], 1.0, 0.0)

    def conv_out(k):
        skip = small_ref[k, 24:25, :]
        group = group_at(here_ref, k, groups)
        return long_ref[group].astype(F32) + skip * conv_ref[group].astype(F32)

    for k in range(groups):
        gated = mask * second_ref[k].astype(F32) * conv_out(k)
        gated_ref[:, k * channels : (k + 1) * channels] = gated.astype(BF16)
    wait_whole(output_ref, sems.at[0])
    mixed = times(gated_ref[...], output_ref[...].reshape(groups * channels, width))
    result_ref[...] = input_ref[...] + mixed + vectors_ref[0:1]
    sums_ref[...] = jnp.zeros_like(sums_ref)

    def norm_step(i, carry):
        part = pl.ds(pl.multiple_of(i * ROW_STEP, ROW_STEP), ROW_STEP)
        values = result_ref[part, :]
        normal, scale = norm_parts(values)
        normal_ref[part, :] = normal
        scale_ref[part, :] = scale
        normed_ref[part, :] = (normal * vectors_ref[1:2] + vectors_ref[2:3]).astype(BF16)
        cot = cot_ref[part, :]
        out_low_ref[part, :] = cot.astype(BF16)
        result_ref[part, :] = values + vectors_ref[3:4]
        hidden_grad_ref[part, :] = jnp.zeros_like(cot)
        sums_ref[0:1, :] += jnp.sum(cot, axis=0, keepdims=True)
        return carry

    lax.fori_loop(0, rows // ROW_STEP, norm_step, 0)
    wait_whole(expand_ref, sems.at[1])
    wait_whole(reduce_ref, sems.at[2])
    per_step = hidden // 2

    def store_units(ref, k, half, values):
        if not sorted_units:
            start = pl.multiple_of((lax.rem(k, 2) * 2 + half) * per_step, per_step)
            ref[k // 2, :, pl.ds(start, per_step)] = values
            return
        share = hidden // 8
        for i in range(4):
            bit0 = (here & 1) ^ (i & 1)
            bit1 = ((here >> 1) & 1) ^ (i >> 1)
            bit2 = ((here >> 2) & 1) ^ half
            outer = jnp.where(k < 2, bit2 * 2 + bit1, bit1 * 2 + bit2)
            start = ((k // 2 * 4 + outer) * 2 + lax.rem(k, 2)) * share
            columns = pl.ds(pl.multiple_of(start, share), share)
            ref[bit0, :, columns] = values[:, i * share : (i + 1) * share]

    def hidden_step(j, carry):
        k, half = j // 2, lax.rem(j, 2)
        units = pl.ds(pl.multiple_of(half * per_step, per_step), per_step)
        expand = expand_ref[k, units, :]
        reduce = reduce_ref[k, units, :]
        value, slope = gelu_parts(contract_cols(normed_ref[...], expand) + bias_ref[j])
        value = value.astype(BF16)
        store_units(act_ref, k, half, value)
        result_ref[...] += times(value, reduce)
        grad = (contract_cols(out_low_ref[...], reduce) * slope).astype(BF16)
        store_units(pre_grad_ref, k, half, grad)
        bias_grad_ref[j] = jnp.sum(grad.astype(F32), axis=0, keepdims=True)
        hidden_grad_ref[...] += times(grad, expand)
        return carry

    lax.fori_loop(0, 2 * groups, hidden_step, 0)
    for copy in stores:
        copy.start()

    def back_step(i, carry):
        part = pl.ds(pl.multiple_of(i * ROW_STEP, ROW_STEP), ROW_STEP)
        res_part, gain_sum, shift_sum = norm_back(
            normal_ref[part, :], scale_ref[part, :], vectors_ref[1:2], hidden_grad_ref[part, :]
        )
        hidden_grad = cot_ref[part, :] + res_part
        hidden_grad_ref[part, :] = hidden_grad
        mix_ref[part, :] = hidden_grad.astype(BF16)
        sums_ref[1:2, :] += gain_sum[None]
        sums_ref[2:3, :] += shift_sum[None]
        sums_ref[3:4, :] += jnp.sum(hidden_grad, axis=0, keepdims=True)
        return carry

    lax.fori_loop(0, rows // ROW_STEP, back_step, 0)
    fold_rows(sums_ref, all_sums_ref)
    for k in range(groups):
        group = group_at(here_ref, k, groups)
        masked_grad = contract_cols(mix_ref[...], output_ref[k]) * mask
        second_grad_ref[k] = (masked_grad * conv_out(k)).astype(BF16)
        conv_grad = (masked_grad * second_ref[k].astype(F32)).astype(BF16)
        conv_grad_ref[group] = conv_grad
        products = conv_grad.astype(F32) * conv_ref[group].astype(F32)
        skip_grad_ref[k] = jnp.sum(products, axis=0, keepdims=True)
    for copy in stores:
        copy.wait()


def grad_shapes(groups, channels, width, split, parts):
    if split:
        return [((2, 2, 2, groups // 2 * parts, channels // 8, width), BF16)] * 2
    return [((groups * parts, channels, width), BF16), ((8, 128), BF16)]


def middle(
    here, long_out, conv_input, second, block_input, cotangent, vectors, small, bias, local, blocks
):
    rows, width = block_input.shape
    groups, _, channels = small.shape
    hidden = local[0].shape[0]
    grouped = ((groups, rows, channels), BF16)
    square = ((rows, width), BF16)
    wide = ((2, rows, groups * hidden // 2), BF16)
    outs = (
        [((rows, width), F32)] * 2
        + [grouped, grouped, square, wide, wide, square, square, square]
        + [((2 * groups, 1, hidden // 2), F32)]
        + [((8 * width // channels, channels), F32), ((groups, 1, channels), F32)]
    )
    return kernel_call(
        functools.partial(middle_kernel, len(blocks), len(blocks) == 8),
        "middle",
        outs,
        [SMEM_SPEC] + [VMEM_SPEC] * 8 + [ANY_SPEC] * (3 + len(blocks)),
        [
            pltpu.VMEM((groups, hidden, width), BF16),
            pltpu.VMEM((groups, hidden, width), BF16),
            pltpu.VMEM((groups, channels, width), BF16),
            pltpu.VMEM((rows, width), F32),
            pltpu.VMEM((rows, 1), F32),
            pltpu.VMEM((8, width), F32),
            pltpu.SemaphoreType.DMA((3,)),
            pltpu.VMEM(wide[0], BF16),
            pltpu.VMEM(wide[0], BF16),
            pltpu.VMEM((rows, width), BF16),
            pltpu.VMEM((rows, width), BF16),
            pltpu.SemaphoreType.DMA((4,)),
        ],
        20_000_000_000,
        48,
        62,
        (
            here,
            long_out,
            conv_input,
            second,
            block_input,
            cotangent,
            vectors,
            small,
            bias,
            *local,
            *blocks,
        ),
        copied=(5, 6, 7, 9),
    )


def leave_kernel(count, here_ref, *refs):
    (
        du_ref,
        conv_grad_ref,
        halo_gates_ref,
        halo_grads_ref,
        small_ref,
        vectors_ref,
        normed_ref,
        gated_ref,
        mix_ref,
        skip_grad_ref,
        bias_grad_ref,
        second_grad_any,
        gates_any,
        projected_any,
        input_any,
        hidden_grad_any,
        local_ref,
    ) = refs[:17]
    blocks = refs[17 : 17 + count]
    input_grad_ref, small_grad_ref, all_sums_ref, *weight_outs = refs[17 + count : 22 + count]
    low_ref, weight_ref, sums_ref, sem, *rest = refs[22 + count :]
    second_grad_ref, gates_ref, projected_ref, input_ref, hidden_grad_ref = rest[:5]
    sems, out_sems = rest[5:7]
    weight_grads = rest[7:]
    rows, width = input_ref.shape
    groups = small_ref.shape[0]
    channels = small_ref.shape[2]
    loads = [
        [
            pltpu.make_async_copy(source.at[k], target.at[k], sems.at[n, k])
            for n, (source, target) in enumerate(
                (
                    (second_grad_any, second_grad_ref),
                    (gates_any, gates_ref),
                    (projected_any, projected_ref),
                )
            )
        ]
        for k in range(groups)
    ]
    late_loads = [
        pltpu.make_async_copy(input_any, input_ref, sems.at[3, 0]),
        pltpu.make_async_copy(hidden_grad_any, hidden_grad_ref, sems.at[3, 1]),
    ]
    for copy in loads[0] + loads[1]:
        copy.start()
    start_input_weights(here_ref, local_ref, blocks, weight_ref, sem)
    for copy in loads[2] + loads[3] + late_loads:
        copy.start()
    row = lax.broadcasted_iota(jnp.int32, (rows + CHUNK, channels), 0)
    ends = (row >= rows) & (here_ref[1] == groups - 1)
    small_grad_ref[...] = jnp.zeros_like(small_grad_ref)

    def keep_grad(k, p, weight_grad):
        if count > 1:
            store_grad(weight_grads, k, k % 2 * 4 + p, here_ref[0], weight_grad)
        else:
            weight_grads[0][4 * k + p] = weight_grad.astype(BF16)

    for k in range(groups):
        nk = (k + 1) % groups
        for copy in loads[k]:
            copy.wait()

        def extended(values, halo):
            return jnp.concatenate([values, halo], axis=0).astype(F32)

        group = group_at(here_ref, k, groups)
        conv_grad = extended(conv_grad_ref[group], halo_grads_ref[0, group])
        skip = small_ref[k, 24:25, :]
        input_side = du_ref[group].astype(F32) + skip * conv_grad
        grads = (
            input_side * extended(gates_ref[k, 1], halo_gates_ref[nk, 1]),
            input_side * extended(gates_ref[k, 0], halo_gates_ref[nk, 0]),
            extended(second_grad_ref[k], halo_grads_ref[1, nk]),
        )
        for p, grad in enumerate(grads):
            grad = jnp.where(ends, 0.0, grad)
            small = small_ref[k, 8 * p : 8 * p + 8, :]
            low = (
                small[1:2] * grad[:rows]
                + small[2:3] * grad[1 : rows + 1]
                + small[3:4] * grad[2 : rows + 2]
            ).astype(BF16)
            low_ref[:, (3 * k + p) * channels : (3 * k + p + 1) * channels] = low
            keep_grad(k, p, contract_rows(low, normed_ref[...]))
            projected = projected_ref[k, p].astype(F32)
            own = grad[:rows]
            small_grad_ref[k, 8 * p : 8 * p + 1, :] = jnp.sum(
                low.astype(F32), axis=0, keepdims=True
            )
            for tap in range(3):
                delayed = projected[CHUNK - tap : rows + CHUNK - tap]
                small_grad_ref[k, 8 * p + 1 + tap : 8 * p + 2 + tap, :] = jnp.sum(
                    own * delayed, axis=0, keepdims=True
                )
            small_grad_ref[k, 8 * p + 4 : 8 * p + 5, :] = jnp.sum(own, axis=0, keepdims=True)
        gated = gated_ref[:, k * channels : (k + 1) * channels]
        keep_grad(k, 3, contract_rows(gated, mix_ref[...]))
        small_grad_ref[k, 24:25, :] = skip_grad_ref[k]
        per_half = bias_grad_ref.shape[2] // channels
        for n in range(2 * per_half):
            bias_row = bias_grad_ref[2 * k + n // per_half]
            first = n % per_half * channels
            small_grad_ref[k, 25 + n : 26 + n, :] = bias_row[:, first : first + channels]
        if count > 1 and k % 2 == 1:
            for n in range(2):
                pltpu.make_async_copy(
                    weight_grads[n].at[k // 2], weight_outs[n].at[k // 2], out_sems.at[n, k // 2]
                ).start()
    if count == 1:
        for n in range(2):
            pltpu.make_async_copy(weight_grads[n], weight_outs[n], out_sems.at[n, 0]).start()
    wait_whole(weight_ref, sem)
    input_grad_ref[...] = times(
        low_ref[...], weight_ref[...].reshape(groups * 3 * channels, width)
    )
    sums_ref[...] = jnp.zeros_like(sums_ref)
    for copy in late_loads:
        copy.wait()

    def back_step(i, carry):
        part = pl.ds(pl.multiple_of(i * ROW_STEP, ROW_STEP), ROW_STEP)
        normal, scale = norm_parts(input_ref[part, :])
        input_part, gain_sum, shift_sum = norm_back(
            normal, scale, vectors_ref[0:1], input_grad_ref[part, :]
        )
        input_grad_ref[part, :] = hidden_grad_ref[part, :] + input_part
        sums_ref[0:1, :] += gain_sum[None]
        sums_ref[1:2, :] += shift_sum[None]
        return carry

    lax.fori_loop(0, rows // ROW_STEP, back_step, 0)
    fold_rows(sums_ref, all_sums_ref)
    for n in range(2):
        if count > 1:
            for half in range(2):
                pltpu.make_async_copy(
                    weight_grads[n].at[half], weight_outs[n].at[half], out_sems.at[n, half]
                ).wait()
        else:
            pltpu.make_async_copy(weight_grads[n], weight_outs[n], out_sems.at[n, 0]).wait()


def leave(
    here,
    conv_input_grad,
    conv_grad,
    second_grad,
    gates,
    projected,
    halo_gates,
    halo_grads,
    small,
    block_input,
    hidden_grad,
    vectors,
    normed,
    gated,
    mix_low,
    skip_grad,
    bias_grad,
    local,
    blocks,
):
    rows, width = block_input.shape
    groups, _, channels = small.shape
    grads = grad_shapes(groups, channels, width, len(blocks) > 1, 4)
    outs = [
        ((rows, width), F32),
        ((groups, SMALL_ROWS, channels), F32),
        ((8 * width // channels, channels), F32),
        *grads,
    ]
    return pl.pallas_call(
        functools.partial(leave_kernel, len(blocks)),
        out_shape=tuple(jax.ShapeDtypeStruct(shape, dtype) for shape, dtype in outs),
        in_specs=[SMEM_SPEC] + [VMEM_SPEC] * 11 + [HBM_SPEC] * 5 + [ANY_SPEC] * (1 + len(blocks)),
        out_specs=(VMEM_SPEC,) * 3 + (HBM_SPEC,) * 2,
        scratch_shapes=[
            pltpu.VMEM((rows, 3 * groups * channels), BF16),
            pltpu.VMEM((groups, 3, channels, width), BF16),
            pltpu.VMEM((8, width), F32),
            pltpu.SemaphoreType.DMA,
            *[
                pltpu.VMEM(a.shape, a.dtype)
                for a in (second_grad, gates, projected, block_input, hidden_grad)
            ],
            pltpu.SemaphoreType.DMA((4, groups)),
            pltpu.SemaphoreType.DMA((2, 2)),
            *[pltpu.VMEM(shape, dtype) for shape, dtype in grads],
        ],
        compiler_params=pltpu.CompilerParams(vmem_limit_bytes=60 << 20),
        cost_estimate=pl.CostEstimate(
            flops=16_000_000_000, bytes_accessed=34 << 20, transcendentals=0
        ),
        name="leave",
    )(
        here,
        conv_input_grad,
        conv_grad,
        halo_gates,
        halo_grads,
        small,
        vectors,
        normed,
        gated,
        mix_low,
        skip_grad,
        bias_grad,
        second_grad,
        gates,
        projected,
        block_input,
        hidden_grad,
        local,
        *blocks,
    )


def per_device(
    block_input,
    lengths,
    mixer_gain,
    mixer_shift,
    input_weight,
    input_bias,
    conv_weight,
    conv_bias,
    enter_weight,
    enter_bias,
    middle_weight,
    middle_bias,
    inner_weight,
    inner_bias,
    frequency,
    filter_weight,
    skip_scale,
    output_weight,
    output_bias,
    feed_gain,
    feed_shift,
    expand_weight,
    expand_bias,
    reduce_weight,
    reduce_bias,
    cotangent,
):
    own_rows, width = block_input.shape
    channels = input_weight.shape[2]
    hidden = expand_weight.shape[1]
    mp_size = lax.axis_size("mp")
    dp_size = lax.axis_size("dp")
    mp_here = lax.axis_index("mp")
    dp_here = lax.axis_index("dp")
    seq_len = own_rows * mp_size
    split = dp_size == 8
    share = hidden // dp_size
    out_share = channels // dp_size
    here = jnp.stack([dp_here, mp_here, lengths[0]]).astype(jnp.int32)

    small_own = jnp.concatenate(
        [
            jnp.concatenate(
                [input_bias[:, None], conv_weight.transpose(1, 0, 2), conv_bias[:, None]]
                + [jnp.zeros((3, 3, channels), F32)],
                axis=1,
            ).reshape(24, channels),
            skip_scale[None],
            expand_bias.reshape(-1, channels),
        ]
    )
    small_own = jnp.pad(small_own, ((0, SMALL_ROWS - small_own.shape[0]), (0, 0)))

    def other_groups(values):
        return jnp.stack([shift_mp(values, k) for k in range(1, mp_size)])

    def turned_groups(stacked, start, sign):
        return jnp.concatenate(
            [
                lax.dynamic_slice_in_dim(stacked, (mp_here + sign * k) % mp_size, 1, 0)
                for k in range(start, mp_size)
            ]
        )

    features = position_features(seq_len, enter_weight.shape[0])
    columns = jnp.stack([enter_bias, middle_bias, inner_bias, frequency], axis=1)
    net_units = frequency.shape[0]
    net_shape = ((3, net_units, seq_len), F32)
    taps_low, *net_values = kernel_call(
        functools.partial(filter_kernel, width),
        "filter_taps",
        [((seq_len, channels), BF16)] + [net_shape] * 3,
        [SMEM_SPEC] + [VMEM_SPEC] * 6,
        [],
        4_000_000_000,
        6,
        32,
        (
            here,
            features,
            jnp.pad(enter_weight, ((0, FEATURE_ROWS - enter_weight.shape[0]), (0, 0))),
            middle_weight,
            inner_weight,
            columns,
            filter_weight,
        ),
    )
    small_rows = jnp.concatenate([small_own, block_input[-CHUNK:].reshape(-1, channels)])
    small_rows = jnp.stack([small_rows] + [shift_mp(small_rows, k) for k in range(1, mp_size)])
    small = small_rows[:, :SMALL_ROWS]
    halo = small_rows[1, SMALL_ROWS:].reshape(CHUNK, width)

    input_turned = input_weight.transpose(1, 2, 0)
    expand_turned = expand_weight.T
    if split:
        input_part = lax.dynamic_slice_in_dim(input_turned, dp_here * out_share, out_share, 1)
        input_pieces = after(other_groups(input_part), small_rows)
        input_blocks = split_blocks(input_pieces, 2, out_share // 2)
    else:
        input_blocks = [other_groups(input_turned)]
    tables = spectral_tables(seq_len)

    if split:
        expand_part = lax.dynamic_slice_in_dim(expand_turned, dp_here * share, share, 0)
        reduce_part = lax.dynamic_slice_in_dim(reduce_weight, dp_here * share, share, 0)
        output_part = lax.dynamic_slice_in_dim(output_weight, dp_here * out_share, out_share, 0)
        half = out_share // 2
        feed_part = jnp.concatenate(
            [expand_part, output_part[:half], reduce_part, output_part[half:]]
        )
        feed_groups = lax.all_gather(after(feed_part, input_pieces), "mp")
    else:
        feed_blocks = [other_groups(w) for w in (output_weight, expand_turned, reduce_weight)]

    mixer_vectors = jnp.stack([mixer_gain, mixer_shift])
    conv_input, second_gate, gates, projected, mixer_normed = enter(
        here,
        block_input,
        halo,
        mixer_vectors,
        small,
        input_turned,
        input_blocks,
    )
    halo_gates = shift_mp(gates[:, :, :CHUNK], -1)

    def exchange(values):
        return lax.all_to_all(values, "mp", 0, 0)

    arrived_input = exchange(conv_input)
    if split:
        feed_pieces = turned_groups(after(feed_groups, conv_input), 1, -1)
        halves = (feed_pieces[:, : share + half], feed_pieces[:, share + half :])
        pairs = [gather_start(part, n, arrived_input) for n, part in enumerate(halves)]
        arrived_input = after(arrived_input, *pairs)
    long_out, spec_u, spec_t = long_conv(tables, arrived_input, taps_low)
    long_out = after(exchange(long_out), halo_gates)
    if split:
        feed_blocks = [
            block for n, pair in enumerate(pairs) for block in gather_rest(pair, n, long_out)
        ]
    vectors = jnp.stack([output_bias, feed_gain, feed_shift, reduce_bias])
    bias = small[:, 25 : 25 + hidden // channels].reshape(2 * mp_size, 1, hidden // 2)
    (
        result,
        hidden_grad,
        conv_grad,
        second_grad,
        gated,
        activated,
        pre_grad,
        feed_normed,
        mix_low,
        out_low,
        bias_grad,
        feed_sums,
        skip_grad,
    ) = middle(
        here,
        long_out,
        conv_input,
        second_gate,
        block_input,
        cotangent,
        vectors,
        small,
        bias,
        (expand_turned, reduce_weight, output_weight),
        feed_blocks,
    )
    halo_grads = shift_mp(jnp.stack([conv_grad[:, :CHUNK], second_grad[:, :CHUNK]]), -1)
    arrived_grad = exchange(conv_grad)

    if split:
        pairs = ((activated, out_low), (pre_grad, feed_normed))
    else:
        def feed_grads(left, right):
            grads = [contract_rows(part, right).astype(BF16) for part in left]
            return own_group(jnp.concatenate(grads).reshape(mp_size, hidden, width))

        reduce_weight_grad = feed_grads(activated, out_low)
        expand_weight_grad = feed_grads(pre_grad, feed_normed).T

    arrived_grad = after(arrived_grad, halo_grads)
    conv_input_grad, taps_grad = long_conv_back(tables, arrived_grad, spec_u, spec_t)
    if split:
        late = [(after(u, taps_grad), right) for u, right in pairs]
        arrived = [
            swap_dp(contract_rows(u[1], right).astype(BF16), 0) for u, right in (pairs[0], late[1])
        ]
        pairs = late
        kept = [
            (contract_rows(u[0], right) + other.astype(F32)).astype(BF16)
            for (u, right), other in zip(pairs, arrived)
        ]
        held = [k.reshape(2, 2, 2, mp_size // 2, share, width) for k in kept]
        first_stages = [
            [jnp.stack([h[n, i] for h in held], axis=1) for i in range(2)] for n in range(2)
        ]
    conv_input_grad = exchange(conv_input_grad)
    if split:
        conv_input_grad = after(
            conv_input_grad, halo_grads, first_stages[0][1], first_stages[1][1]
        )
    input_grad, small_grad, mixer_sums, grads_kept, grads_away = leave(
        here,
        conv_input_grad,
        conv_grad,
        second_grad,
        gates,
        projected,
        halo_gates,
        halo_grads,
        small,
        block_input,
        hidden_grad,
        mixer_vectors,
        mixer_normed,
        gated,
        mix_low,
        skip_grad,
        bias_grad,
        input_turned,
        input_blocks,
    )
    if split:
        held = (grads_kept.astype(F32) + swap_dp(grads_away, 0).astype(F32)).astype(BF16)
        taps_grad = after(taps_grad, held)
    else:
        taps_grad = after(taps_grad, grads_kept)
    net_grads, filter_weight_grad = kernel_call(
        functools.partial(filter_back_kernel, width),
        "filter_back",
        [((net_units, 4 * net_units), F32), ((net_units, channels), F32)],
        [SMEM_SPEC] + [VMEM_SPEC] * 9,
        [pltpu.VMEM((net_units, seq_len), F32)],
        8_000_000_000,
        6,
        32,
        (
            here,
            features,
            middle_weight,
            inner_weight,
            columns,
            filter_weight,
            *net_values,
            taps_grad,
        ),
    )
    packed = [net_grads, feed_sums, mixer_sums, filter_weight_grad]
    packed.append(small_grad.reshape(-1, channels))
    ends = [sum(p.shape[0] for p in packed[:n]) for n in range(len(packed) + 1)]
    packed = jnp.concatenate(packed)
    def small_sums(summed):
        by_group = summed[ends[4] :].reshape(mp_size, SMALL_ROWS, channels)
        return sum_groups(
            [jnp.concatenate([summed[: ends[3]], by_group[k]]) for k in range(mp_size)]
        )

    if split:
        stages = [
            add_across(part, bit, small_grad) for part, bit in zip(first_stages, (2, 1))
        ]
        stages = [add_across(part, bit) for part, bit in zip(stages, (1, 2))]
        feed_grads = jnp.concatenate(stages, axis=1).transpose(1, 0, 2, 3)
        feed_grads = turned_groups(feed_grads, 0, -1).reshape(-1, width)
        feed_total = lax.psum_scatter(feed_grads, "mp", scatter_dimension=0, tiled=True)
        held = [add_across(held[0], 2, net_grads), add_across(held[1], 1, net_grads)]
        packed = after(packed, *held)
        held = [add_across(held[0], 1), add_across(held[1], 2)]
        feed_total = after(feed_total, *held)
        mine = jnp.concatenate(held).reshape(mp_size, 4, out_share, width)
        mine = turned_groups(mine, 0, -1).reshape(-1, width)
        input_total = lax.psum_scatter(mine, "mp", scatter_dimension=0, tiled=True)
        input_total = input_total.reshape(4, out_share, width)
        reduce_total, expand_total = feed_total[:share], feed_total[share:]
        summed = sum_dp(packed)
        blocks = []
        for n, total in enumerate((expand_total, reduce_total)):
            blocks.extend(gather_rest(gather_start(total.astype(BF16), n), n))
        expand_weight_grad, reduce_weight_grad = kernel_call(
            place_feed_kernel,
            "place_feed",
            [((width, hidden), F32), ((hidden, width), F32)],
            [SMEM_SPEC] + [VMEM_SPEC] * len(blocks),
            [],
            0,
            14,
            32,
            (here, *blocks),
        )
        input_total = after(input_total, expand_weight_grad)
        along_mp = small_sums(after(summed, input_total))
        blocks = split_blocks(input_total, 1, out_share // 2)
        input_weight_grad, output_weight_grad = kernel_call(
            place_input_kernel,
            "place_input",
            [((3, width, channels), F32), ((channels, width), F32)],
            [SMEM_SPEC] + [VMEM_SPEC] * len(blocks),
            [pltpu.VMEM((3, channels, width), F32)],
            0,
            8,
            24,
            (here, *blocks),
        )
        input_weight_grad = input_weight_grad.transpose(1, 0, 2)
    else:
        input_total = own_group(grads_kept.reshape(mp_size, 4, channels, width))
        input_weight_grad = input_total[:3].transpose(2, 0, 1)
        output_weight_grad = input_total[3]
        summed = sum_dp(packed)
        along_mp = small_sums(summed)

    everywhere, groups_sum = along_mp[: ends[3]], along_mp[ends[3] :]
    net = everywhere[: ends[1]]
    net_bias = net[:, 3 * net_units :].T
    feed_sums = unfold_rows(everywhere[ends[1] : ends[2]])
    mixer_sums = unfold_rows(everywhere[ends[2] : ends[3]])
    parts = groups_sum[:24].reshape(3, 8, channels)
    return (
        result,
        input_grad,
        mixer_sums[0],
        mixer_sums[1],
        input_weight_grad,
        parts[:, 0],
        parts[:, 1:4].transpose(1, 0, 2),
        parts[:, 4],
        net[: enter_weight.shape[0], :net_units],
        net_bias[0],
        net[:, net_units : 2 * net_units],
        net_bias[1],
        net[:, 2 * net_units : 3 * net_units],
        net_bias[2],
        net_bias[3],
        summed[ends[3] : ends[4]],
        groups_sum[24],
        output_weight_grad,
        feed_sums[3],
        feed_sums[1],
        feed_sums[2],
        expand_weight_grad,
        groups_sum[25 : 25 + hidden // channels].reshape(hidden),
        reduce_weight_grad,
        feed_sums[0],
    )


ROWS = P(("dp", "mp"), None)
FIRST = P("mp", None)
SECOND = P(None, "mp")
THIRD = P(None, None, "mp")


def solution(mesh):
    return jax.shard_map(
        per_device,
        mesh=mesh,
        in_specs=(
            ROWS, P("dp"), P(), P(), THIRD, SECOND, THIRD, SECOND,
            P(), P(), P(), P(), P(), P(), P(), SECOND,
            P("mp"), FIRST, P(), P(), P(), SECOND, P("mp"), FIRST, P(), ROWS,
        ),
        out_specs=(
            ROWS, ROWS, P(), P(), THIRD, SECOND, THIRD, SECOND,
            P(), P(), P(), P(), P(), P(), P(), SECOND,
            P("mp"), FIRST, P(), P(), P(), SECOND, P("mp"), FIRST, P(),
        ),
        check_vma=False,
    )
```

profile of v0, /device:TPU:1, one launch (start us, length us, event | category | flops | bytes accessed | tf_op | source)
XLA Modules:
  0.0 508.2 jit_solution(15986186804018346869)
XLA Ops:
  10.4 3.2 collective-permute-start.1
  15.1 1.7 copy.87
  16.8 2.9 collective-permute-start.5
  19.8 3.9 copy.89
  28.5 10.8 %collective-permute-done.4 = bf16[3,32,1024]{2,1,0:T(8,128)(2,1)S(1)} collective-permute-done((bf16[3,32,1024]{2,1,0:T(8,128)(2,1)S(1)}, bf16[3,32,1024]{2,1,0:T(8,128)(2,1)S(1)}, u32[]{:S(2)}, u32[]{:S(2)}) %collective-permute-start.4) | collective-permute-done | bytes 196640 | tf_op jit(solution)/shard_map/ppermute | solution.py:350
  42.1 4.8 collective-permute-done.6
  49.6 2.7 collective-permute-start.8
  52.4 7.8 %collective-permute-done.7.refs_1_.refs_18_ = bf16[2,3,3,16,1024]{4,3,2,1,0:T(8,128)(2,1)S(1)} collective-permute-done((bf16[2,3,3,16,1024]{4,3,2,1,0:T(8,128)(2,1)S(1)}, bf16[2,3,3,16,1024]{4,3,2,1,0:T(8,128)(2,1)S(1)}, u32[]{:S(2)}, u32[]{:S(2)}) %collective-permute-start.7) | collective-permute-done | bytes 589856 | tf_op jit(solution)/shard_map/ppermute | solution.py:355
  60.1 2.8 collective-permute-start.9
  69.1 12.6 %enter.1 = (bf16[4,512,256]{2,1,0:T(8,128)(2,1)}, bf16[4,512,256]{2,1,0:T(8,128)(2,1)S(1)}, bf16[4,2,512,256]{3,2,1,0:T(8,128)(2,1)S(1)}, bf16[4,3,528,256]{3,2,1,0:T(8,128)(2,1)}, bf16[512,1024]{1,0:T(8,128)(2,1)S(1)}) custom-call(s32[3]{0:T(128)S(1)} %pad_add_fusion.here_ref, f32[512,1024]{1,0:T(8,128)S(1)} %copy-done.7, ...), custom_call_target="tpu_custom_call" | custom-call | flops 3221225472 | bytes 16777216 | tf_op jit(solution)/shard_map/enter/pallas_call | solution.py:292
  85.0 5.4 %all-to-all-start = ((bf16[4,512,256]{2,1,0:T(8,128)(2,1)}), bf16[4,512,256]{2,1,0:T(8,128)(2,1)S(1)}, u32[]{:S(2)}, u32[]{:S(2)}) async-start(bf16[4,512,256]{2,1,0:T(8,128)(2,1)} %get-tuple-element.86.refs_1_), calls=%async_computation | async-start | bytes 2097152 | tf_op jit(solution)/shard_map/all_to_all | solution.py:1164
  96.4 8.6 %filter_taps.1 = (bf16[2048,256]{1,0:T(8,128)(2,1)S(1)}, f32[3,64,2048]{2,1,0:T(8,128)S(1)}, f32[3,64,2048]{2,1,0:T(8,128)S(1)}, f32[3,64,2048]{2,1,0:T(8,128)S(1)}) custom-call(s32[3]{0:T(128)S(1)} %pad_add_fusion.here_ref, f32[40,2048]{1,0:T(8,128)S(1)} %copy-done.24, f32[40,64]{1,0:T(8,128)S(1)} %pad.9.enter_ref, f32[64,64]{1,0:T(8,128)S(1)} %copy-done.11, ...), custom_call_target="tpu_custom_call" | custom-call | flops 4000000000 | bytes 6291456 | tf_op jit(solution)/shard_map/filter_taps/pallas_call | solution.py:292
  109.5 6.5 %all-to-all-done = bf16[4,512,256]{2,1,0:T(8,128)(2,1)S(1)} async-done(((bf16[4,512,256]{2,1,0:T(8,128)(2,1)}), bf16[4,512,256]{2,1,0:T(8,128)(2,1)S(1)}, u32[]{:S(2)}, u32[]{:S(2)}) %all-to-all-start) | async-done | bytes 1048608 | tf_op jit(solution)/shard_map/all_to_all | solution.py:1164
  116.0 2.7 pad_maximum_fusion.6.refs_11_
  119.5 3.0 pad_maximum_fusion.7.refs_15_
  123.2 13.9 %long_conv.1 = (bf16[32,64,256]{2,1,0:T(8,128)(2,1)}, bf16[64,64,256]{2,1,0:T(8,128)(2,1)S(1)}, bf16[64,64,256]{2,1,0:T(8,128)(2,1)S(1)}) custom-call(bf16[1024,512]{1,0:T(8,128)(2,1)S(1)} %copy-done.20, bf16[32,128,128]{2,1,0:T(8,128)(2,1)S(1)} %copy-done.18, bf16[32,128,128]{2,1,0:T(8,128)(2,1)S(1)} %copy-done.16, bf16[512,1024]{1,0:T(8,128)(2,1)S(1)} %copy-done.15, ...), custom_call_target="tpu_custom_call" | custom-call | flops 8999999488 | bytes 14680064 | tf_op jit(solution)/shard_map/long_conv/pallas_call | solution.py:292
  139.7 4.4 all-to-all-start.1
  145.0 3.2 collective-permute-start.16
  148.2 2.4 collective-permute-start.18
  150.6 10.5 %collective-permute-done.16.refs_2_ = bf16[4,2,16,256]{3,2,1,0:T(8,128)(2,1)S(1)} collective-permute-done((bf16[4,2,16,256]{3,2,1,0:T(8,128)(2,1)S(1)}, bf16[4,2,16,256]{3,2,1,0:T(8,128)(2,1)S(1)}, u32[]{:S(2)}, u32[]{:S(2)}) %collective-permute-start.16) | collective-permute-done | bytes 65568 | tf_op jit(solution)/shard_map/ppermute | solution.py:350
  161.1 8.3 %all-to-all-done.1.refs_0_ = bf16[4,512,256]{2,1,0:T(8,128)(2,1)} async-done(((bf16[4,512,256]{2,1,0:T(8,128)(2,1)}), bf16[4,512,256]{2,1,0:T(8,128)(2,1)}, u32[]{:S(2)}, u32[]{:S(2)}) %all-to-all-start.1) | async-done | bytes 1048608 | tf_op jit(solution)/shard_map/all_to_all | solution.py:1164
  169.4 2.2 collective-permute-start.19
  175.3 2.5 collective-permute-done.22.refs_18_
  177.8 44.5 %middle.1 = (f32[512,1024]{1,0:T(8,128)}, f32[512,1024]{1,0:T(8,128)}, bf16[4,512,256]{2,1,0:T(8,128)(2,1)}, bf16[4,512,256]{2,1,0:T(8,128)(2,1)}, bf16[512,1024...) custom-call(s32[3]{0:T(128)} %copy-done.5, ...), custom_call_target="tpu_custom_call" | custom-call | flops 20000000000 | bytes 50331648 | tf_op jit(solution)/shard_map/middle/pallas_call | solution.py:292
  222.3 3.5 all-to-all-start.2
  226.7 3.3 collective-permute-start.23
  229.9 6.3 %convolution_convert_fusion.1 = bf16[2048,1024]{1,0:T(8,128)(2,1)} fusion(bf16[512,1024]{1,0:T(8,128)(2,1)} %get-tuple-element.109, bf16[2,512,2048]{2,1,0:T(8,128)(2,1)} %get-tuple-element.108), kind=kOutput, calls=%fused_computation.7 | convolution fusion | flops 2149580800 | bytes 7340032 | tf_op jit(solution)/shard_map/dot_general | solution.py:446
  237.1 7.2 %collective-permute-done.23.refs_3_ = bf16[2,4,16,256]{3,2,1,0:T(8,128)(2,1)S(1)} collective-permute-done((bf16[2,4,16,256]{3,2,1,0:T(8,128)(2,1)S(1)}, bf16[2,4,16,256]{3,2,1,0:T(8,128)(2,1)S(1)}, u32[]{:S(2)}, u32[]{:S(2)}) %collective-permute-start.23) | collective-permute-done | bytes 65568 | tf_op jit(solution)/shard_map/ppermute | solution.py:350
  244.3 6.9 %all-to-all-done.2 = bf16[4,512,256]{2,1,0:T(8,128)(2,1)S(1)} async-done(((bf16[4,512,256]{2,1,0:T(8,128)(2,1)}), bf16[4,512,256]{2,1,0:T(8,128)(2,1)S(1)}, u32[]{:S(2)}, u32[]{:S(2)}) %all-to-all-start.2) | async-done | bytes 1048608 | tf_op jit(solution)/shard_map/all_to_all | solution.py:1164
  258.1 13.6 %long_conv_back.1 = (bf16[4,528,256]{2,1,0:T(8,128)(2,1)}, f32[32,64,256]{2,1,0:T(8,128)S(1)}) custom-call(bf16[1024,512]{1,0:T(8,128)(2,1)S(1)} %copy-done.21, bf16[32,128,128]{2,1,0:T(8,128)(2,1)S(1)} %copy-done.19, bf16[32,128,128]{2,1,0:T(8,128)(2,1)S(1)} %copy-done.17, bf16[512,1024]{1,0:T(8,128)(2,1)S(1)} %copy-done.15, ...), custom_call_target="tpu_custom_call" | custom-call | flops 8999999488 | bytes 14680064 | tf_op jit(solution)/shard_map/long_conv_back/pallas_call | solution.py:292
  271.8 4.4 convolution_convert_fusion
  276.1 1.9 collective-permute-start.25
  278.0 4.3 all-to-all-start.3
  282.6 5.2 %add_convert_fusion.2 = bf16[2048,1024]{1,0:T(8,128)(2,1)S(1)} fusion(bf16[2048,1024]{1,0:T(8,128)(2,1)} %collective-permute-done.24, bf16[512,1024]{1,0:T(8,128)(2,1)S(1)} %copy-done.61, bf16[2,512,2048]{2,1,0:T(8,128)(2,1)} %get-tuple-element.108), kind=kOutput, calls=%fused_computation.2 | convolution fusion | flops 2153775104 | bytes 11534336 | tf_op jit(solution)/shard_map/dot_general | solution.py:446
  290.3 4.6 add_convert_fusion.1
  294.9 1.8 slice_bitcast_fusion.2
  301.3 7.5 %all-to-all-done.3.refs_0_ = bf16[4,528,256]{2,1,0:T(8,128)(2,1)} async-done(((bf16[4,528,256]{2,1,0:T(8,128)(2,1)}), bf16[4,528,256]{2,1,0:T(8,128)(2,1)}, u32[]{:S(2)}, u32[]{:S(2)}) %all-to-all-start.3) | async-done | bytes 1081376 | tf_op jit(solution)/shard_map/all_to_all | solution.py:1164
  308.8 24.9 %leave.1 = (f32[512,1024]{1,0:T(8,128)}, f32[4,32,256]{2,1,0:T(8,128)}, f32[32,256]{1,0:T(8,128)}, bf16[2,2,2,8,32,1024]{5,4,3,2,1,0:T(8,128)(2,1)}, bf16[2,2,2,8,32,1024]{5,4,3,2,1,0:T(8,128)(2,1)}) custom-call(s32[3]{0:T(128)} %copy-done.5, bf16[4,528,256]{2,1,0:T(8,128)(2,1)} %all-to-all-done.3.refs_0_, bf16[4,512,256]{2,1,0:T(8,128)(2,1)} %get-tuple-element.100.refs_1_, ...), custom_call_target="tpu_custom_call" | custom-call | flops 16000000000 | bytes 35651584 | tf_op jit(solution)/shard_map/leave/pallas_call | solution.py:990
  336.5 9.1 %collective-permute-done.34 = bf16[2,2,2,128,1024]{4,3,2,1,0:T(8,128)(2,1)} collective-permute-done((bf16[2,2,2,128,1024]{4,3,2,1,0:T(8,128)(2,1)}, bf16[2,2,2,128,1024]{4,3,2,1,0:T(8,128)(2,1)}, u32[]{:S(2)}, u32[]{:S(2)}) %collective-permute-start.34) | collective-permute-done | bytes 2097184 | tf_op jit(solution)/shard_map/ppermute | solution.py:355
  345.6 2.6 fusion
  350.4 2.6 add_convert_fusion.3
  355.1 18.1 %collective-permute-done.35 = bf16[2,2,128,1024]{3,2,1,0:T(8,128)(2,1)S(1)} collective-permute-done((bf16[2,2,128,1024]{3,2,1,0:T(8,128)(2,1)}, bf16[2,2,128,1024]{3,2,1,0:T(8,128)(2,1)S(1)}, u32[]{:S(2)}, u32[]{:S(2)}) %collective-permute-start.35) | collective-permute-done | bytes 1048608 | tf_op jit(solution)/shard_map/ppermute | solution.py:355
  374.8 3.4 collective-permute-done.37
  381.3 5.6 %add_convert_fusion = bf16[2,2,2,8,32,1024]{5,4,3,2,1,0:T(8,128)(2,1)S(1)} fusion(bf16[2,2,2,8,32,1024]{5,4,3,2,1,0:T(8,128)(2,1)} %collective-permute-done.26, bf16[2,2,2,8,32,1024]{5,4,3,2,1,0:T(8,128)(2,1)} %get-tuple-element.125), kind=kLoop, calls=%fused_computation | loop fusion | flops 8388608 | bytes 12582912 | tf_op jit(solution)/shard_map/convert_element_type | solution.py:1263
  390.4 5.9 %filter_back.1 = (f32[64,256]{1,0:T(8,128)S(1)}, f32[64,256]{1,0:T(8,128)S(1)}) custom-call(s32[3]{0:T(128)S(1)} %copy-done.6, f32[40,2048]{1,0:T(8,128)S(1)} %copy-done.24, f32[64,64]{1,0:T(8,128)S(1)} %copy-done.11, f32[64,64]{1,0:T(8,128)S(1)} %copy-done.12, f32[64,4]{1,0:T(8,128)S(1)} %copy.90.columns_ref, f32[64,256]{1,0:T(8,128)S(1)} %copy-done.10, ...), custom_call_target="tpu_custom_call" | custom-call | flops 8000000000 | bytes 6291456 | tf_op jit(solution)/shard_map/filter_back/pallas_call | solution.py:292
  396.3 14.0 %collective-permute-done.28 = bf16[2,8,32,1024]{3,2,1,0:T(8,128)(2,1)S(1)} collective-permute-done((bf16[2,8,32,1024]{3,2,1,0:T(8,128)(2,1)S(1)}, bf16[2,8,32,1024]{3,2,1,0:T(8,128)(2,1)S(1)}, u32[]{:S(2)}, u32[]{:S(2)}) %collective-permute-start.28) | collective-permute-done | bytes 1048608 | tf_op jit(solution)/shard_map/ppermute | solution.py:355
  412.5 8.9 %collective-permute-done.33 = bf16[8,32,1024]{2,1,0:T(8,128)(2,1)S(1)} collective-permute-done((bf16[8,32,1024]{2,1,0:T(8,128)(2,1)S(1)}, bf16[8,32,1024]{2,1,0:T(8,128)(2,1)S(1)}, u32[]{:S(2)}, u32[]{:S(2)}) %collective-permute-start.33) | collective-permute-done | bytes 524320 | tf_op jit(solution)/shard_map/ppermute | solution.py:355
  423.7 2.2 reduce-scatter.5.cloned.1.call-done
  429.5 3.5 collective-permute-done.38
  433.0 1.8 collective-permute-start.39
  434.9 1.8 collective-permute-start.43
  436.7 2.4 collective-permute-start.29
  441.4 4.0 collective-permute-done.39.refs_1_
  445.4 5.4 %collective-permute-start.41 = (bf16[2,128,1024]{2,1,0:T(8,128)(2,1)S(1)}, bf16[2,128,1024]{2,1,0:T(8,128)(2,1)S(1)}, u32[]{:S(2)}, u32[]{:S(2)}) collective-permute-start(bf16[2,128,1024]{2,1,0:T(8,128)(2,1)S(1)} %collective-permute-done.39.refs_1_), channel_id=1, source_target_pairs={{0,4},{4,0},{8,12},{12,8},{16,20},{20,16},{24,28},{28,24},{1,5},{5... | collective-permute-start | bytes 1572872 | tf_op jit(solution)/shard_map/ppermute | solution.py:355
  453.7 5.1 %collective-permute-done.31 = f32[320,256]{1,0:T(8,128)S(1)} collective-permute-done((f32[320,256]{1,0:T(8,128)S(1)}, f32[320,256]{1,0:T(8,128)S(1)}, u32[]{:S(2)}, u32[]{:S(2)}) %collective-permute-start.31) | collective-permute-done | bytes 327712 | tf_op jit(solution)/shard_map/ppermute | solution.py:355
  459.5 4.7 place_feed.1
  466.4 2.3 collective-permute-start.53
  468.9 2.3 collective-permute-start.47
  472.5 4.8 collective-permute-start.51
  477.4 3.0 collective-permute-start.55
  481.8 3.4 collective-permute-done.50.refs_1_
  485.2 3.4 collective-permute-start.52
  488.6 4.6 collective-permute-start.56
  498.1 3.4 place_input.1
  (303 shorter events, 97.5 us)
Async XLA Ops:
  7.2 83.7 %all-gather.3.cloned.1.call-start = ((), (), s32[]{:S(2)}) async-start(), calls=%async_computation.8 | async-start | bytes 2949120 | tf_op jit(solution)/shard_map/all_gather | solution.py:1147
  10.4 16.0 %collective-permute-start.1 = (f32[96,256]{1,0:T(8,128)S(1)}, f32[96,256]{1,0:T(8,128)S(1)}, u32[]{:S(2)}, u32[]{:S(2)}) collective-permute-start(f32[96,256]{1,0:T(8,128)S(1)} %get-tuple-element.201), channel_id=1, source_target_pairs={{0,2},{1,3},{2,0},{3,1},{4,6},{5,7},{6,4},{7,5},{8,10},{9,11},{10,... | collective-permute-start | bytes 294920 | tf_op jit(solution)/shard_map/ppermute | solution.py:350
  13.6 14.1 %collective-permute-start.2 = (f32[96,256]{1,0:T(8,128)S(1)}, f32[96,256]{1,0:T(8,128)S(1)}, u32[]{:S(2)}, u32[]{:S(2)}) collective-permute-start(f32[96,256]{1,0:T(8,128)S(1)} %get-tuple-element.201), channel_id=1, source_target_pairs={{0,3},{1,0},{2,1},{3,2},{4,7},{5,4},{6,5},{7,6},{8,11},{9,8},{10,9... | collective-permute-start | bytes 294920 | tf_op jit(solution)/shard_map/ppermute | solution.py:350
  14.7 13.0 %collective-permute-start = (f32[96,256]{1,0:T(8,128)S(1)}, f32[96,256]{1,0:T(8,128)S(1)}, u32[]{:S(2)}, u32[]{:S(2)}) collective-permute-start(f32[96,256]{1,0:T(8,128)S(1)} %get-tuple-element.201), channel_id=1, source_target_pairs={{0,1},{1,2},{2,3},{3,0},{4,5},{5,6},{6,7},{7,4},{8,9},{9,10},{10,1... | collective-permute-start | bytes 294920 | tf_op jit(solution)/shard_map/ppermute | solution.py:350
  16.8 11.7 %collective-permute-start.5 = (bf16[3,32,1024]{2,1,0:T(8,128)(2,1)S(1)}, bf16[3,32,1024]{2,1,0:T(8,128)(2,1)S(1)}, u32[]{:S(2)}, u32[]{:S(2)}) collective-permute-start(bf16[3,32,1024]{2,1,0:T(8,128)(2,1)S(1)} %dynamic-slice_bitcast_fusion.1), channel_id=1, source_target_pairs={{0,3},{1,0},{2,1},{3,2},{4,7},{5,4},{6,5},{7,6},{8,11},{9,8},{10,9... | collective-permute-start | bytes 589832 | tf_op jit(solution)/shard_map/ppermute | solution.py:350
  19.8 19.6 %collective-permute-start.4 = (bf16[3,32,1024]{2,1,0:T(8,128)(2,1)S(1)}, bf16[3,32,1024]{2,1,0:T(8,128)(2,1)S(1)}, u32[]{:S(2)}, u32[]{:S(2)}) collective-permute-start(bf16[3,32,1024]{2,1,0:T(8,128)(2,1)S(1)} %dynamic-slice_bitcast_fusion.1), channel_id=1, source_target_pairs={{0,2},{1,3},{2,0},{3,1},{4,6},{5,7},{6,4},{7,5},{8,10},{9,11},{10,... | collective-permute-start | bytes 589832 | tf_op jit(solution)/shard_map/ppermute | solution.py:350
  26.4 12.9 %collective-permute-start.3 = (bf16[3,32,1024]{2,1,0:T(8,128)(2,1)S(1)}, bf16[3,32,1024]{2,1,0:T(8,128)(2,1)S(1)}, u32[]{:S(2)}, u32[]{:S(2)}) collective-permute-start(bf16[3,32,1024]{2,1,0:T(8,128)(2,1)S(1)} %dynamic-slice_bitcast_fusion.1), channel_id=1, source_target_pairs={{0,1},{1,2},{2,3},{3,0},{4,5},{5,6},{6,7},{7,4},{8,9},{9,10},{10,1... | collective-permute-start | bytes 589832 | tf_op jit(solution)/shard_map/ppermute | solution.py:350
  39.6 7.3 %collective-permute-start.6 = (bf16[3,3,16,1024]{3,2,1,0:T(8,128)(2,1)S(1)}, bf16[3,3,16,1024]{3,2,1,0:T(8,128)(2,1)S(1)}, u32[]{:S(2)}, u32[]{:S(2)}) collective-permute-start(bf16[3,3,16,1024]{3,2,1,0:T(8,128)(2,1)S(1)} %get-tuple-element.177), channel_id=1, source_target_pairs={{0,16},{4,20},{8,24},{12,28},{16,0},{20,4},{24,8},{28,12},{1,17},{... | collective-permute-start | bytes 884744 | tf_op jit(solution)/shard_map/ppermute | solution.py:355
  40.9 7.3 %collective-permute-start.10 = (bf16[3,3,16,1024]{3,2,1,0:T(8,128)(2,1)S(1)}, bf16[3,3,16,1024]{3,2,1,0:T(8,128)(2,1)S(1)}, u32[]{:S(2)}, u32[]{:S(2)}) collective-permute-start(bf16[3,3,16,1024]{3,2,1,0:T(8,128)(2,1)S(1)} %get-tuple-element.176), channel_id=1, source_target_pairs={{0,8},{4,12},{8,0},{12,4},{16,24},{20,28},{24,16},{28,20},{1,9},{5... | collective-permute-start | bytes 884744 | tf_op jit(solution)/shard_map/ppermute | solution.py:355
  47.0 13.1 %collective-permute-start.7 = (bf16[2,3,3,16,1024]{4,3,2,1,0:T(8,128)(2,1)S(1)}, bf16[2,3,3,16,1024]{4,3,2,1,0:T(8,128)(2,1)S(1)}, u32[]{:S(2)}, u32[]{:S(2)}) collective-permute-start(bf16[2,3,3,16,1024]{4,3,2,1,0:T(8,128)(2,1)S(1)} %pad_maximum_fusion.11.refs_0_.refs_17_), channel_id=1, source_target_pairs={{0,8},{4,12},{8,0},{12,4},{16,24},{20,28},{24,16},{28,20},{1,9},{5... | collective-permute-start | bytes 1769480 | tf_op jit(solution)/shard_map/ppermute | solution.py:355
  48.3 14.7 %collective-permute-start.11 = (bf16[2,3,3,16,1024]{4,3,2,1,0:T(8,128)(2,1)S(1)}, bf16[2,3,3,16,1024]{4,3,2,1,0:T(8,128)(2,1)}, u32[]{:S(2)}, u32[]{:S(2)}) collective-permute-start(bf16[2,3,3,16,1024]{4,3,2,1,0:T(8,128)(2,1)S(1)} %pad_maximum_fusion.12.refs_4_.refs_21_), channel_id=1, source_target_pairs={{0,16},{4,20},{8,24},{12,28},{16,0},{20,4},{24,8},{28,12},{1,17},{... | collective-permute-start | bytes 1769480 | tf_op jit(solution)/shard_map/ppermute | solution.py:355
  49.6 17.9 %collective-permute-start.8 = (bf16[2,3,3,16,1024]{4,3,2,1,0:T(8,128)(2,1)S(1)}, bf16[2,3,3,16,1024]{4,3,2,1,0:T(8,128)(2,1)}, u32[]{:S(2)}, u32[]{:S(2)}) collective-permute-start(bf16[2,3,3,16,1024]{4,3,2,1,0:T(8,128)(2,1)S(1)} %pad_maximum_fusion.11.refs_0_.refs_17_), channel_id=1, source_target_pairs={{0,4},{4,0},{8,12},{12,8},{16,20},{20,16},{24,28},{28,24},{1,5},{5... | collective-permute-start | bytes 1769480 | tf_op jit(solution)/shard_map/ppermute | solution.py:355
  52.4 15.1 %collective-permute-start.12 = (bf16[2,3,3,16,1024]{4,3,2,1,0:T(8,128)(2,1)S(1)}, bf16[2,3,3,16,1024]{4,3,2,1,0:T(8,128)(2,1)}, u32[]{:S(2)}, u32[]{:S(2)}) collective-permute-start(bf16[2,3,3,16,1024]{4,3,2,1,0:T(8,128)(2,1)S(1)} %pad_maximum_fusion.12.refs_4_.refs_21_), channel_id=1, source_target_pairs={{0,4},{4,0},{8,12},{12,8},{16,20},{20,16},{24,28},{28,24},{1,5},{5... | collective-permute-start | bytes 1769480 | tf_op jit(solution)/shard_map/ppermute | solution.py:355
  60.1 7.4 %collective-permute-start.9 = (bf16[2,3,3,16,1024]{4,3,2,1,0:T(8,128)(2,1)S(1)}, bf16[2,3,3,16,1024]{4,3,2,1,0:T(8,128)(2,1)}, u32[]{:S(2)}, u32[]{:S(2)}) collective-permute-start(bf16[2,3,3,16,1024]{4,3,2,1,0:T(8,128)(2,1)S(1)} %collective-permute-done.7.refs_1_.refs_18_), channel_id=1, source_target_pairs={{0,4},{4,0},{8,12},{12,8},{16,20},{20,16},{24,28},{28,24},{1,5},{5... | collective-permute-start | bytes 1769480 | tf_op jit(solution)/shard_map/ppermute | solution.py:355
  63.0 4.5 collective-permute-start.13
  85.0 31.0 %all-to-all-start = ((bf16[4,512,256]{2,1,0:T(8,128)(2,1)}), bf16[4,512,256]{2,1,0:T(8,128)(2,1)S(1)}, u32[]{:S(2)}, u32[]{:S(2)}) async-start(bf16[4,512,256]{2,1,0:T(8,128)(2,1)} %get-tuple-element.86.refs_1_), calls=%async_computation | async-start | bytes 2097152 | tf_op jit(solution)/shard_map/all_to_all | solution.py:1164
  93.8 22.2 %collective-permute-start.14 = (bf16[3,144,1024]{2,1,0:T(8,128)(2,1)S(1)}, bf16[3,144,1024]{2,1,0:T(8,128)(2,1)}, u32[]{:S(2)}, u32[]{:S(2)}) collective-permute-start(bf16[3,144,1024]{2,1,0:T(8,128)(2,1)S(1)} %get-tuple-element.89), channel_id=1, source_target_pairs={{0,16},{4,20},{8,24},{12,28},{16,0},{20,4},{24,8},{28,12},{1,17},{... | collective-permute-start | bytes 2654216 | tf_op jit(solution)/shard_map/ppermute | solution.py:355
  95.0 24.5 %collective-permute-start.15 = (bf16[3,144,1024]{2,1,0:T(8,128)(2,1)}, bf16[3,144,1024]{2,1,0:T(8,128)(2,1)}, u32[]{:S(2)}, u32[]{:S(2)}) collective-permute-start(bf16[3,144,1024]{2,1,0:T(8,128)(2,1)} %get-tuple-element.90), channel_id=1, source_target_pairs={{0,8},{4,12},{8,0},{12,4},{16,24},{20,28},{24,16},{28,20},{1,9},{5... | collective-permute-start | bytes 2654216 | tf_op jit(solution)/shard_map/ppermute | solution.py:355
  118.7 50.7 %collective-permute-start.17 = (bf16[2,3,144,1024]{3,2,1,0:T(8,128)(2,1)}, bf16[2,3,144,1024]{3,2,1,0:T(8,128)(2,1)}, u32[]{:S(2)}, u32[]{:S(2)}) collective-permute-start(bf16[2,3,144,1024]{3,2,1,0:T(8,128)(2,1)} %pad_maximum_fusion.6.refs_11_), channel_id=1, source_target_pairs={{0,8},{4,12},{8,0},{12,4},{16,24},{20,28},{24,16},{28,20},{1,9},{5... | collective-permute-start | bytes 5308424 | tf_op jit(solution)/shard_map/ppermute | solution.py:355
  122.4 47.0 %collective-permute-start.20 = (bf16[2,3,144,1024]{3,2,1,0:T(8,128)(2,1)}, bf16[2,3,144,1024]{3,2,1,0:T(8,128)(2,1)}, u32[]{:S(2)}, u32[]{:S(2)}) collective-permute-start(bf16[2,3,144,1024]{3,2,1,0:T(8,128)(2,1)} %pad_maximum_fusion.7.refs_15_), channel_id=1, source_target_pairs={{0,16},{4,20},{8,24},{12,28},{16,0},{20,4},{24,8},{28,12},{1,17},{... | collective-permute-start | bytes 5308424 | tf_op jit(solution)/shard_map/ppermute | solution.py:355
  139.7 29.7 %all-to-all-start.1 = ((bf16[4,512,256]{2,1,0:T(8,128)(2,1)}), bf16[4,512,256]{2,1,0:T(8,128)(2,1)}, u32[]{:S(2)}, u32[]{:S(2)}) async-start(bf16[4,512,256]{2,1,0:T(8,128)(2,1)} %bitcast.34), calls=%async_computation.1 | async-start | bytes 2097152 | tf_op jit(solution)/shard_map/all_to_all | solution.py:1164
  145.0 16.1 %collective-permute-start.16 = (bf16[4,2,16,256]{3,2,1,0:T(8,128)(2,1)S(1)}, bf16[4,2,16,256]{3,2,1,0:T(8,128)(2,1)S(1)}, u32[]{:S(2)}, u32[]{:S(2)}) collective-permute-start(bf16[4,2,16,256]{3,2,1,0:T(8,128)(2,1)S(1)} %slice.258), channel_id=1, source_target_pairs={{0,3},{1,0},{2,1},{3,2},{4,7},{5,4},{6,5},{7,6},{8,11},{9,8},{10,9... | collective-permute-start | bytes 196616 | tf_op jit(solution)/shard_map/ppermute | solution.py:350
  148.2 25.5 %collective-permute-start.18 = (bf16[2,3,144,1024]{3,2,1,0:T(8,128)(2,1)}, bf16[2,3,144,1024]{3,2,1,0:T(8,128)(2,1)}, u32[]{:S(2)}, u32[]{:S(2)}) collective-permute-start(bf16[2,3,144,1024]{3,2,1,0:T(8,128)(2,1)} %pad_maximum_fusion.6.refs_11_), channel_id=1, source_target_pairs={{0,4},{4,0},{8,12},{12,8},{16,20},{20,16},{24,28},{28,24},{1,5},{5... | collective-permute-start | bytes 5308424 | tf_op jit(solution)/shard_map/ppermute | solution.py:355
  150.6 23.1 %collective-permute-start.21 = (bf16[2,3,144,1024]{3,2,1,0:T(8,128)(2,1)}, bf16[2,3,144,1024]{3,2,1,0:T(8,128)(2,1)}, u32[]{:S(2)}, u32[]{:S(2)}) collective-permute-start(bf16[2,3,144,1024]{3,2,1,0:T(8,128)(2,1)} %pad_maximum_fusion.7.refs_15_), channel_id=1, source_target_pairs={{0,4},{4,0},{8,12},{12,8},{16,20},{20,16},{24,28},{28,24},{1,5},{5... | collective-permute-start | bytes 5308424 | tf_op jit(solution)/shard_map/ppermute | solution.py:355
  169.4 5.8 %collective-permute-start.19 = (bf16[2,3,144,1024]{3,2,1,0:T(8,128)(2,1)}, bf16[2,3,144,1024]{3,2,1,0:T(8,128)(2,1)}, u32[]{:S(2)}, u32[]{:S(2)}) collective-permute-start(bf16[2,3,144,1024]{3,2,1,0:T(8,128)(2,1)} %collective-permute-done.17.refs_12_), channel_id=1, source_target_pairs={{0,4},{4,0},{8,12},{12,8},{16,20},{20,16},{24,28},{28,24},{1,5},{5... | collective-permute-start | bytes 5308424 | tf_op jit(solution)/shard_map/ppermute | solution.py:355
  171.6 6.2 %collective-permute-start.22 = (bf16[2,3,144,1024]{3,2,1,0:T(8,128)(2,1)}, bf16[2,3,144,1024]{3,2,1,0:T(8,128)(2,1)}, u32[]{:S(2)}, u32[]{:S(2)}) collective-permute-start(bf16[2,3,144,1024]{3,2,1,0:T(8,128)(2,1)} %collective-permute-done.20.refs_16_), channel_id=1, source_target_pairs={{0,4},{4,0},{8,12},{12,8},{16,20},{20,16},{24,28},{28,24},{1,5},{5... | collective-permute-start | bytes 5308424 | tf_op jit(solution)/shard_map/ppermute | solution.py:355
  222.3 29.0 %all-to-all-start.2 = ((bf16[4,512,256]{2,1,0:T(8,128)(2,1)}), bf16[4,512,256]{2,1,0:T(8,128)(2,1)S(1)}, u32[]{:S(2)}, u32[]{:S(2)}) async-start(bf16[4,512,256]{2,1,0:T(8,128)(2,1)} %get-tuple-element.100.refs_1_), calls=%async_computation.2 | async-start | bytes 2097152 | tf_op jit(solution)/shard_map/all_to_all | solution.py:1164
  226.7 17.7 %collective-permute-start.23 = (bf16[2,4,16,256]{3,2,1,0:T(8,128)(2,1)S(1)}, bf16[2,4,16,256]{3,2,1,0:T(8,128)(2,1)S(1)}, u32[]{:S(2)}, u32[]{:S(2)}) collective-permute-start(bf16[2,4,16,256]{3,2,1,0:T(8,128)(2,1)S(1)} %pad_maximum_fusion.24), channel_id=1, source_target_pairs={{0,3},{1,0},{2,1},{3,2},{4,7},{5,4},{6,5},{7,6},{8,11},{9,8},{10,9... | collective-permute-start | bytes 196616 | tf_op jit(solution)/shard_map/ppermute | solution.py:350
  236.2 46.3 %collective-permute-start.24 = (bf16[2048,1024]{1,0:T(8,128)(2,1)}, bf16[2048,1024]{1,0:T(8,128)(2,1)}, u32[]{:S(2)}, u32[]{:S(2)}) collective-permute-start(bf16[2048,1024]{1,0:T(8,128)(2,1)} %convolution_convert_fusion.1), channel_id=1, source_target_pairs={{0,4},{4,0},{8,12},{12,8},{16,20},{20,16},{24,28},{28,24},{1,5},{5... | collective-permute-start | bytes 12582920 | tf_op jit(solution)/shard_map/ppermute | solution.py:355
  276.1 12.1 %collective-permute-start.25 = (bf16[2048,1024]{1,0:T(8,128)(2,1)}, bf16[2048,1024]{1,0:T(8,128)(2,1)}, u32[]{:S(2)}, u32[]{:S(2)}) collective-permute-start(bf16[2048,1024]{1,0:T(8,128)(2,1)} %convolution_convert_fusion), channel_id=1, source_target_pairs={{0,4},{4,0},{8,12},{12,8},{16,20},{20,16},{24,28},{28,24},{1,5},{5... | collective-permute-start | bytes 12582920 | tf_op jit(solution)/shard_map/ppermute | solution.py:355
  278.0 30.7 %all-to-all-start.3 = ((bf16[4,528,256]{2,1,0:T(8,128)(2,1)}), bf16[4,528,256]{2,1,0:T(8,128)(2,1)}, u32[]{:S(2)}, u32[]{:S(2)}) async-start(bf16[4,528,256]{2,1,0:T(8,128)(2,1)} %get-tuple-element.105), calls=%async_computation.3 | async-start | bytes 2162688 | tf_op jit(solution)/shard_map/all_to_all | solution.py:1164
  282.3 143.6 %reduce-scatter.5.cloned.1.call-start = ((), (), s32[]{:S(2)}) async-start(), calls=%async_computation.7 | async-start | bytes 2621440 | tf_op jit(solution)/shard_map/reduce_scatter | solution.py:1304
  298.2 47.4 %collective-permute-start.34 = (bf16[2,2,2,128,1024]{4,3,2,1,0:T(8,128)(2,1)}, bf16[2,2,2,128,1024]{4,3,2,1,0:T(8,128)(2,1)}, u32[]{:S(2)}, u32[]{:S(2)}) collective-permute-start(bf16[2,2,2,128,1024]{4,3,2,1,0:T(8,128)(2,1)} %pad_maximum_fusion), channel_id=1, source_target_pairs={{0,16},{4,20},{8,24},{12,28},{16,0},{20,4},{24,8},{28,12},{1,17},{... | collective-permute-start | bytes 6291464 | tf_op jit(solution)/shard_map/ppermute | solution.py:355
  300.5 49.9 %collective-permute-start.36 = (bf16[2,2,2,128,1024]{4,3,2,0,1:T(8,128)(2,1)}, bf16[2,2,2,128,1024]{4,3,2,0,1:T(8,128)(2,1)}, u32[]{:S(2)}, u32[]{:S(2)}) collective-permute-start(bf16[2,2,2,128,1024]{4,3,2,0,1:T(8,128)(2,1)} %pad_maximum_fusion.1), channel_id=1, source_target_pairs={{0,8},{4,12},{8,0},{12,4},{16,24},{20,28},{24,16},{28,20},{1,9},{5... | collective-permute-start | bytes 6291464 | tf_op jit(solution)/shard_map/ppermute | solution.py:355
  333.7 47.6 %collective-permute-start.26 = (bf16[2,2,2,8,32,1024]{5,4,3,2,1,0:T(8,128)(2,1)}, bf16[2,2,2,8,32,1024]{5,4,3,2,1,0:T(8,128)(2,1)}, u32[]{:S(2)}, u32[]{:S(2)}) collective-permute-start(bf16[2,2,2,8,32,1024]{5,4,3,2,1,0:T(8,128)(2,1)} %get-tuple-element.126), channel_id=1, source_target_pairs={{0,4},{4,0},{8,12},{12,8},{16,20},{20,16},{24,28},{28,24},{1,5},{5... | collective-permute-start | bytes 12582920 | tf_op jit(solution)/shard_map/ppermute | solution.py:355
  349.3 23.9 %collective-permute-start.35 = (bf16[2,2,128,1024]{3,2,1,0:T(8,128)(2,1)}, bf16[2,2,128,1024]{3,2,1,0:T(8,128)(2,1)S(1)}, u32[]{:S(2)}, u32[]{:S(2)}) collective-permute-start(bf16[2,2,128,1024]{3,2,1,0:T(8,128)(2,1)} %slice_bitcast_fusion.4), channel_id=1, source_target_pairs={{0,8},{4,12},{8,0},{12,4},{16,24},{20,28},{24,16},{28,20},{1,9},{5... | collective-permute-start | bytes 3145736 | tf_op jit(solution)/shard_map/ppermute | solution.py:355
  354.7 23.6 %collective-permute-start.37 = (bf16[2,2,128,1024]{3,2,1,0:T(8,128)(2,1)}, bf16[2,2,128,1024]{3,2,1,0:T(8,128)(2,1)S(1)}, u32[]{:S(2)}, u32[]{:S(2)}) collective-permute-start(bf16[2,2,128,1024]{3,2,1,0:T(8,128)(2,1)} %slice_bitcast_fusion), channel_id=1, source_target_pairs={{0,16},{4,20},{8,24},{12,28},{16,0},{20,4},{24,8},{28,12},{1,17},{... | collective-permute-start | bytes 3145736 | tf_op jit(solution)/shard_map/ppermute | solution.py:355
  381.1 83.1 %reduce-scatter.3.cloned.1.call-start = ((), (), s32[]{:S(2)}) async-start(), calls=%async_computation.6 | async-start | bytes 1310720 | tf_op jit(solution)/shard_map/reduce_scatter | solution.py:1311
  387.6 22.7 %collective-permute-start.28 = (bf16[2,8,32,1024]{3,2,1,0:T(8,128)(2,1)S(1)}, bf16[2,8,32,1024]{3,2,1,0:T(8,128)(2,1)S(1)}, u32[]{:S(2)}, u32[]{:S(2)}) collective-permute-start(bf16[2,8,32,1024]{3,2,1,0:T(8,128)(2,1)S(1)} %get-tuple-element.158), channel_id=1, source_target_pairs={{0,8},{4,12},{8,0},{12,4},{16,24},{20,28},{24,16},{28,20},{1,9},{5... | collective-permute-start | bytes 3145736 | tf_op jit(solution)/shard_map/ppermute | solution.py:355
  388.0 23.2 %collective-permute-start.27 = (bf16[2,8,32,1024]{3,2,1,0:T(8,128)(2,1)S(1)}, bf16[2,8,32,1024]{3,2,1,0:T(8,128)(2,1)S(1)}, u32[]{:S(2)}, u32[]{:S(2)}) collective-permute-start(bf16[2,8,32,1024]{3,2,1,0:T(8,128)(2,1)S(1)} %get-tuple-element.159), channel_id=1, source_target_pairs={{0,16},{4,20},{8,24},{12,28},{16,0},{20,4},{24,8},{28,12},{1,17},{... | collective-permute-start | bytes 3145736 | tf_op jit(solution)/shard_map/ppermute | solution.py:355
  410.8 10.6 %collective-permute-start.33 = (bf16[8,32,1024]{2,1,0:T(8,128)(2,1)S(1)}, bf16[8,32,1024]{2,1,0:T(8,128)(2,1)S(1)}, u32[]{:S(2)}, u32[]{:S(2)}) collective-permute-start(bf16[8,32,1024]{2,1,0:T(8,128)(2,1)S(1)} %slice_bitcast_fusion.16), channel_id=1, source_target_pairs={{0,16},{4,20},{8,24},{12,28},{16,0},{20,4},{24,8},{28,12},{1,17},{... | collective-permute-start | bytes 1572872 | tf_op jit(solution)/shard_map/ppermute | solution.py:355
  411.7 10.3 %collective-permute-start.32 = (bf16[8,32,1024]{2,1,0:T(8,128)(2,1)S(1)}, bf16[8,32,1024]{2,1,0:T(8,128)(2,1)S(1)}, u32[]{:S(2)}, u32[]{:S(2)}) collective-permute-start(bf16[8,32,1024]{2,1,0:T(8,128)(2,1)S(1)} %slice_bitcast_fusion.18), channel_id=1, source_target_pairs={{0,8},{4,12},{8,0},{12,4},{16,24},{20,28},{24,16},{28,20},{1,9},{5... | collective-permute-start | bytes 1572872 | tf_op jit(solution)/shard_map/ppermute | solution.py:355
  427.0 6.0 %collective-permute-start.38 = (bf16[128,1024]{1,0:T(8,128)(2,1)S(1)}, bf16[128,1024]{1,0:T(8,128)(2,1)S(1)}, u32[]{:S(2)}, u32[]{:S(2)}) collective-permute-start(bf16[128,1024]{1,0:T(8,128)(2,1)S(1)} %get-tuple-element.181), channel_id=1, source_target_pairs={{0,16},{4,20},{8,24},{12,28},{16,0},{20,4},{24,8},{28,12},{1,17},{... | collective-permute-start | bytes 786440 | tf_op jit(solution)/shard_map/ppermute | solution.py:355
  428.3 6.5 %collective-permute-start.42 = (bf16[128,1024]{1,0:T(8,128)(2,1)S(1)}, bf16[128,1024]{1,0:T(8,128)(2,1)S(1)}, u32[]{:S(2)}, u32[]{:S(2)}) collective-permute-start(bf16[128,1024]{1,0:T(8,128)(2,1)S(1)} %get-tuple-element.180), channel_id=1, source_target_pairs={{0,8},{4,12},{8,0},{12,4},{16,24},{20,28},{24,16},{28,20},{1,9},{5... | collective-permute-start | bytes 786440 | tf_op jit(solution)/shard_map/ppermute | solution.py:355
  433.0 12.4 %collective-permute-start.39 = (bf16[2,128,1024]{2,1,0:T(8,128)(2,1)S(1)}, bf16[2,128,1024]{2,1,0:T(8,128)(2,1)S(1)}, u32[]{:S(2)}, u32[]{:S(2)}) collective-permute-start(bf16[2,128,1024]{2,1,0:T(8,128)(2,1)S(1)} %pad_maximum_fusion.14.refs_0_), channel_id=1, source_target_pairs={{0,8},{4,12},{8,0},{12,4},{16,24},{20,28},{24,16},{28,20},{1,9},{5... | collective-permute-start | bytes 1572872 | tf_op jit(solution)/shard_map/ppermute | solution.py:355
  434.9 15.9 %collective-permute-start.43 = (bf16[2,128,1024]{2,1,0:T(8,128)(2,1)S(1)}, bf16[2,128,1024]{2,1,0:T(8,128)(2,1)S(1)}, u32[]{:S(2)}, u32[]{:S(2)}) collective-permute-start(bf16[2,128,1024]{2,1,0:T(8,128)(2,1)S(1)} %pad_maximum_fusion.15.refs_4_), channel_id=1, source_target_pairs={{0,16},{4,20},{8,24},{12,28},{16,0},{20,4},{24,8},{28,12},{1,17},{... | collective-permute-start | bytes 1572872 | tf_op jit(solution)/shard_map/ppermute | solution.py:355
  436.7 3.6 collective-permute-start.29
  440.4 12.0 %collective-permute-start.30 = (f32[320,256]{1,0:T(8,128)S(1)}, f32[320,256]{1,0:T(8,128)S(1)}, u32[]{:S(2)}, u32[]{:S(2)}) collective-permute-start(f32[320,256]{1,0:T(8,128)S(1)} %add.137), channel_id=1, source_target_pairs={{0,8},{4,12},{8,0},{12,4},{16,24},{20,28},{24,16},{28,20},{1,9},{5... | collective-permute-start | bytes 983048 | tf_op jit(solution)/shard_map/ppermute | solution.py:355
  440.7 18.7 %collective-permute-start.40 = (bf16[2,128,1024]{2,1,0:T(8,128)(2,1)S(1)}, bf16[2,128,1024]{2,1,0:T(8,128)(2,1)S(1)}, u32[]{:S(2)}, u32[]{:S(2)}) collective-permute-start(bf16[2,128,1024]{2,1,0:T(8,128)(2,1)S(1)} %pad_maximum_fusion.14.refs_0_), channel_id=1, source_target_pairs={{0,4},{4,0},{8,12},{12,8},{16,20},{20,16},{24,28},{28,24},{1,5},{5... | collective-permute-start | bytes 1572872 | tf_op jit(solution)/shard_map/ppermute | solution.py:355
  441.4 18.0 %collective-permute-start.44 = (bf16[2,128,1024]{2,1,0:T(8,128)(2,1)S(1)}, bf16[2,128,1024]{2,1,0:T(8,128)(2,1)S(1)}, u32[]{:S(2)}, u32[]{:S(2)}) collective-permute-start(bf16[2,128,1024]{2,1,0:T(8,128)(2,1)S(1)} %pad_maximum_fusion.15.refs_4_), channel_id=1, source_target_pairs={{0,4},{4,0},{8,12},{12,8},{16,20},{20,16},{24,28},{28,24},{1,5},{5... | collective-permute-start | bytes 1572872 | tf_op jit(solution)/shard_map/ppermute | solution.py:355
  445.4 14.0 %collective-permute-start.41 = (bf16[2,128,1024]{2,1,0:T(8,128)(2,1)S(1)}, bf16[2,128,1024]{2,1,0:T(8,128)(2,1)S(1)}, u32[]{:S(2)}, u32[]{:S(2)}) collective-permute-start(bf16[2,128,1024]{2,1,0:T(8,128)(2,1)S(1)} %collective-permute-done.39.refs_1_), channel_id=1, source_target_pairs={{0,4},{4,0},{8,12},{12,8},{16,20},{20,16},{24,28},{28,24},{1,5},{5... | collective-permute-start | bytes 1572872 | tf_op jit(solution)/shard_map/ppermute | solution.py:355
  450.8 8.6 %collective-permute-start.45 = (bf16[2,128,1024]{2,1,0:T(8,128)(2,1)S(1)}, bf16[2,128,1024]{2,1,0:T(8,128)(2,1)S(1)}, u32[]{:S(2)}, u32[]{:S(2)}) collective-permute-start(bf16[2,128,1024]{2,1,0:T(8,128)(2,1)S(1)} %collective-permute-done.43.refs_5_), channel_id=1, source_target_pairs={{0,4},{4,0},{8,12},{12,8},{16,20},{20,16},{24,28},{28,24},{1,5},{5... | collective-permute-start | bytes 1572872 | tf_op jit(solution)/shard_map/ppermute | solution.py:355
  452.4 6.3 %collective-permute-start.31 = (f32[320,256]{1,0:T(8,128)S(1)}, f32[320,256]{1,0:T(8,128)S(1)}, u32[]{:S(2)}, u32[]{:S(2)}) collective-permute-start(f32[320,256]{1,0:T(8,128)S(1)} %add.138), channel_id=1, source_target_pairs={{0,16},{4,20},{8,24},{12,28},{16,0},{20,4},{24,8},{28,12},{1,17},{... | collective-permute-start | bytes 983048 | tf_op jit(solution)/shard_map/ppermute | solution.py:355
  465.2 7.3 %collective-permute-start.49 = (bf16[4,16,1024]{2,1,0:T(8,128)(2,1)S(1)}, bf16[4,16,1024]{2,1,0:T(8,128)(2,1)S(1)}, u32[]{:S(2)}, u32[]{:S(2)}) collective-permute-start(bf16[4,16,1024]{2,1,0:T(8,128)(2,1)S(1)} %get-tuple-element.191), channel_id=1, source_target_pairs={{0,16},{4,20},{8,24},{12,28},{16,0},{20,4},{24,8},{28,12},{1,17},{... | collective-permute-start | bytes 393224 | tf_op jit(solution)/shard_map/ppermute | solution.py:355
  466.4 10.9 %collective-permute-start.53 = (bf16[4,16,1024]{2,1,0:T(8,128)(2,1)S(1)}, bf16[4,16,1024]{2,1,0:T(8,128)(2,1)S(1)}, u32[]{:S(2)}, u32[]{:S(2)}) collective-permute-start(bf16[4,16,1024]{2,1,0:T(8,128)(2,1)S(1)} %get-tuple-element.190), channel_id=1, source_target_pairs={{0,8},{4,12},{8,0},{12,4},{16,24},{20,28},{24,16},{28,20},{1,9},{5... | collective-permute-start | bytes 393224 | tf_op jit(solution)/shard_map/ppermute | solution.py:355
  468.8 8.6 %collective-permute-start.46 = (f32[160,256]{1,0:T(8,128)S(1)}, f32[160,256]{1,0:T(8,128)S(1)}, u32[]{:S(2)}, u32[]{:S(2)}) collective-permute-start(f32[160,256]{1,0:T(8,128)S(1)} %get-tuple-element.197), channel_id=1, source_target_pairs={{0,3},{1,0},{2,1},{3,2},{4,7},{5,4},{6,5},{7,6},{8,11},{9,8},{10,9... | collective-permute-start | bytes 491528 | tf_op jit(solution)/shard_map/ppermute | solution.py:350
  468.9 11.6 %collective-permute-start.47 = (f32[160,256]{1,0:T(8,128)S(1)}, f32[160,256]{1,0:T(8,128)S(1)}, u32[]{:S(2)}, u32[]{:S(2)}) collective-permute-start(f32[160,256]{1,0:T(8,128)S(1)} %get-tuple-element.198), channel_id=1, source_target_pairs={{0,2},{1,3},{2,0},{3,1},{4,6},{5,7},{6,4},{7,5},{8,10},{9,11},{10,... | collective-permute-start | bytes 491528 | tf_op jit(solution)/shard_map/ppermute | solution.py:350
  471.1 9.3 %collective-permute-start.48 = (f32[160,256]{1,0:T(8,128)S(1)}, f32[160,256]{1,0:T(8,128)S(1)}, u32[]{:S(2)}, u32[]{:S(2)}) collective-permute-start(f32[160,256]{1,0:T(8,128)S(1)} %get-tuple-element.199), channel_id=1, source_target_pairs={{0,1},{1,2},{2,3},{3,0},{4,5},{5,6},{6,7},{7,4},{8,9},{9,10},{10,1... | collective-permute-start | bytes 491528 | tf_op jit(solution)/shard_map/ppermute | solution.py:350
  472.5 25.5 %collective-permute-start.51 = (bf16[2,4,16,1024]{3,2,1,0:T(8,128)(2,1)S(1)}, bf16[2,4,16,1024]{3,2,1,0:T(8,128)(2,1)S(1)}, u32[]{:S(2)}, u32[]{:S(2)}) collective-permute-start(bf16[2,4,16,1024]{3,2,1,0:T(8,128)(2,1)S(1)} %pad_maximum_fusion.17.refs_0_), channel_id=1, source_target_pairs={{0,4},{4,0},{8,12},{12,8},{16,20},{20,16},{24,28},{28,24},{1,5},{5... | collective-permute-start | bytes 786440 | tf_op jit(solution)/shard_map/ppermute | solution.py:355
  477.3 7.9 %collective-permute-start.50 = (bf16[2,4,16,1024]{3,2,1,0:T(8,128)(2,1)S(1)}, bf16[2,4,16,1024]{3,2,1,0:T(8,128)(2,1)S(1)}, u32[]{:S(2)}, u32[]{:S(2)}) collective-permute-start(bf16[2,4,16,1024]{3,2,1,0:T(8,128)(2,1)S(1)} %pad_maximum_fusion.17.refs_0_), channel_id=1, source_target_pairs={{0,8},{4,12},{8,0},{12,4},{16,24},{20,28},{24,16},{28,20},{1,9},{5... | collective-permute-start | bytes 786440 | tf_op jit(solution)/shard_map/ppermute | solution.py:355
  477.4 20.7 %collective-permute-start.55 = (bf16[2,4,16,1024]{3,2,1,0:T(8,128)(2,1)S(1)}, bf16[2,4,16,1024]{3,2,1,0:T(8,128)(2,1)S(1)}, u32[]{:S(2)}, u32[]{:S(2)}) collective-permute-start(bf16[2,4,16,1024]{3,2,1,0:T(8,128)(2,1)S(1)} %pad_maximum_fusion.18.refs_4_), channel_id=1, source_target_pairs={{0,4},{4,0},{8,12},{12,8},{16,20},{20,16},{24,28},{28,24},{1,5},{5... | collective-permute-start | bytes 786440 | tf_op jit(solution)/shard_map/ppermute | solution.py:355
  480.4 8.2 %collective-permute-start.54 = (bf16[2,4,16,1024]{3,2,1,0:T(8,128)(2,1)S(1)}, bf16[2,4,16,1024]{3,2,1,0:T(8,128)(2,1)S(1)}, u32[]{:S(2)}, u32[]{:S(2)}) collective-permute-start(bf16[2,4,16,1024]{3,2,1,0:T(8,128)(2,1)S(1)} %pad_maximum_fusion.18.refs_4_), channel_id=1, source_target_pairs={{0,16},{4,20},{8,24},{12,28},{16,0},{20,4},{24,8},{28,12},{1,17},{... | collective-permute-start | bytes 786440 | tf_op jit(solution)/shard_map/ppermute | solution.py:355
  485.2 12.8 %collective-permute-start.52 = (bf16[2,4,16,1024]{3,2,1,0:T(8,128)(2,1)S(1)}, bf16[2,4,16,1024]{3,2,1,0:T(8,128)(2,1)S(1)}, u32[]{:S(2)}, u32[]{:S(2)}) collective-permute-start(bf16[2,4,16,1024]{3,2,1,0:T(8,128)(2,1)S(1)} %collective-permute-done.50.refs_1_), channel_id=1, source_target_pairs={{0,4},{4,0},{8,12},{12,8},{16,20},{20,16},{24,28},{28,24},{1,5},{5... | collective-permute-start | bytes 786440 | tf_op jit(solution)/shard_map/ppermute | solution.py:355
  488.6 9.5 %collective-permute-start.56 = (bf16[2,4,16,1024]{3,2,1,0:T(8,128)(2,1)S(1)}, bf16[2,4,16,1024]{3,2,1,0:T(8,128)(2,1)S(1)}, u32[]{:S(2)}, u32[]{:S(2)}) collective-permute-start(bf16[2,4,16,1024]{3,2,1,0:T(8,128)(2,1)S(1)} %collective-permute-done.54.refs_5_), channel_id=1, source_target_pairs={{0,4},{4,0},{8,12},{12,8},{16,20},{20,16},{24,28},{28,24},{1,5},{5... | collective-permute-start | bytes 786440 | tf_op jit(solution)/shard_map/ppermute | solution.py:355
  (62 other events, 662.2 us)
Sparse Core Ops, SparseCore 0:
  39.5 51.3 all-gather.2
  381.2 44.6 reduce-scatter.4
  428.9 26.4 reduce-scatter.2
where the time goes:
time: 516 us; the launch traced here: 508 us
  waiting for transfers between devices  150 us (29%)
  Pallas kernels  132 us (26%)
  starting transfers between devices  101 us (20%)
  local copies, waits for them, and re-layouts  55.9 us (11%)
  other arithmetic  32.5 us (6%)
  matrix products  20.5 us (4%)
  between operations  15.7 us (3%)
    pallas_call x8, Pallas kernels, kernel_call(): pl.pallas_call(kernel, out_shape=tuple((jax.ShapeDtypeStruct(shape, dtype...  107 us
    ppermute x46, waiting for transfers between devices, swap_dp(): lax.ppermute(values_in, 'dp', [(i, i ^ 1 << bit) for i in range(size)])  89.6 us
    ppermute x46, starting transfers between devices, swap_dp(): lax.ppermute(values_in, 'dp', [(i, i ^ 1 << bit) for i in range(size)])  65.2 us
    unnamed x135, local copies, waits for them, and re-layouts  31.2 us
    all_to_all x4, waiting for transfers between devices, exchange(): return lax.all_to_all(values, 'mp', 0, 0)  29.3 us
    ppermute x11, waiting for transfers between devices, shift_mp(): lax.ppermute(values_in, 'mp', [(i, (i + count) % size) for i in range(siz...  28.5 us
    pallas_call x1, Pallas kernels, leave(): pl.pallas_call(functools.partial(leave_kernel, len(blocks)), out_shape=tu...  24.9 us
    dot_general x4, matrix products, contract_rows(): lax.dot_general(left, right, (((0,), (0,)), ((), ())), preferred_element_...  20.5 us
  transfers between devices with their start and end apart: 64, of which 25 were waited for; matrix products, arithmetic and copies ran while one was open for 16% of the time, Pallas kernels for 17%

commit v1 on v0

--- a/solution.py
+++ b/solution.py
@@ -509,14 +509,8 @@
 
 def enter_kernel(count, here_ref, input_ref, halo_ref, vectors_ref, small_ref, local_ref, *refs):
     blocks = refs[:count]
-    outs = refs[count : count + 5]
-    weight_ref, rows_ref, sem, *results, out_sems = refs[count + 5 :]
-    conv_input_ref, second_ref, gates_ref, projected_ref, normed_ref = results
-
-    def store(n, k):
-        return pltpu.make_async_copy(results[n].at[k], outs[n].at[k], out_sems.at[n, k])
-
-    store_normed = pltpu.make_async_copy(normed_ref, outs[4], out_sems.at[4, 0])
+    conv_input_ref, second_ref, gates_ref, projected_ref, normed_ref = refs[count : count + 5]
+    weight_ref, rows_ref, sem = refs[count + 5 :]
     rows = input_ref.shape[0]
     groups, _, channels = conv_input_ref.shape
     start_input_weights(here_ref, local_ref, blocks, weight_ref, sem)
@@ -534,7 +528,6 @@
         return carry
 
     lax.fori_loop(0, rows // ROW_STEP, norm_step, 0)
-    store_normed.start()
     wait_whole(weight_ref, sem)
     row = lax.broadcasted_iota(jnp.int32, (rows + CHUNK, channels), 0)
     begins = (row < CHUNK) & (here_ref[1] == 0)
@@ -556,12 +549,6 @@
         gates_ref[k, 0] = mixed[0].astype(BF16)
         gates_ref[k, 1] = mixed[1].astype(BF16)
         second_ref[k] = mixed[2].astype(BF16)
-        for n in range(4):
-            store(n, group if n == 0 else k).start()
-    store_normed.wait()
-    for k in range(groups):
-        for n in range(4):
-            store(n, k).wait()
 
 
 def enter(here, block_input, halo, vectors, small, local, blocks):
@@ -584,14 +571,11 @@
             pltpu.VMEM((groups, parts, channels, width), BF16),
             pltpu.VMEM((rows + CHUNK, width), BF16),
             pltpu.SemaphoreType.DMA,
-            *[pltpu.VMEM(shape, dtype) for shape, dtype in outs],
-            pltpu.SemaphoreType.DMA((5, groups)),
         ],
         2 * rows * width * parts * groups * channels,
         16,
         40,
         (here, block_input, halo, vectors, small, local, *blocks),
-        copied=(0, 1, 2, 3, 4),
     )
 
 
@@ -1328,7 +1312,7 @@
         )
         input_total = after(input_total, expand_weight_grad)
         along_mp = small_sums(after(summed, input_total))
-        blocks = split_blocks(input_total, 1, out_share // 2)
+        blocks = split_blocks(input_total, 1, out_share // 2, along_mp)
         input_weight_grad, output_weight_grad = kernel_call(
             place_input_kernel,
             "place_input",

time: 516 us -> 515 us (level)
  transfers between devices with their start and end apart: 64 -> 64, of which waited for: 25 -> 25; matrix products, arithmetic and copies ran while one was open for 16% -> 16% of each run, Pallas kernels for 17% -> 16%
where the time goes in v1:
time: 515 us; the launch traced here: 508 us
  waiting for transfers between devices  150 us (29%)
  Pallas kernels  132 us (26%)
  starting transfers between devices  101 us (20%)
  local copies, waits for them, and re-layouts  55.9 us (11%)
  other arithmetic  32.5 us (6%)
  matrix products  20.5 us (4%)
  between operations  15.7 us (3%)
    pallas_call x8, Pallas kernels, kernel_call(): pl.pallas_call(kernel, out_shape=tuple((jax.ShapeDtypeStruct(shape, dtype...  107 us
    ppermute x46, waiting for transfers between devices, swap_dp(): lax.ppermute(values_in, 'dp', [(i, i ^ 1 << bit) for i in range(size)])  89.7 us
    ppermute x46, starting transfers between devices, swap_dp(): lax.ppermute(values_in, 'dp', [(i, i ^ 1 << bit) for i in range(size)])  65.2 us
    unnamed x135, local copies, waits for them, and re-layouts  31.2 us
    all_to_all x4, waiting for transfers between devices, exchange(): return lax.all_to_all(values, 'mp', 0, 0)  28.9 us
    ppermute x11, waiting for transfers between devices, shift_mp(): lax.ppermute(values_in, 'mp', [(i, (i + count) % size) for i in range(siz...  28.3 us
    pallas_call x1, Pallas kernels, leave(): pl.pallas_call(functools.partial(leave_kernel, len(blocks)), out_shape=tu...  24.9 us
    dot_general x4, matrix products, contract_rows(): lax.dot_general(left, right, (((0,), (0,)), ((), ())), preferred_element_...  20.5 us
  transfers between devices with their start and end apart: 64, of which 25 were waited for; matrix products, arithmetic and copies ran while one was open for 16% of the time, Pallas kernels for 16%

profile of v1, /device:TPU:1, one launch (start us, length us, event | category | flops | bytes accessed | tf_op | source)
XLA Modules:
  0.0 507.6 jit_solution(17493380466287283383)
XLA Ops:
  10.4 3.2 collective-permute-start.1
  15.1 1.7 copy.87
  16.8 2.9 collective-permute-start.5
  19.8 3.9 copy.89
  28.5 10.8 %collective-permute-done.4 = bf16[3,32,1024]{2,1,0:T(8,128)(2,1)S(1)} collective-permute-done((bf16[3,32,1024]{2,1,0:T(8,128)(2,1)S(1)}, bf16[3,32,1024]{2,1,0:T(8,128)(2,1)S(1)}, u32[]{:S(2)}, u32[]{:S(2)}) %collective-permute-start.4) | collective-permute-done | bytes 196640 | tf_op jit(solution)/shard_map/ppermute | solution.py:350
  42.1 4.8 collective-permute-done.6
  49.6 2.7 collective-permute-start.8
  52.4 7.8 %collective-permute-done.7.refs_1_.refs_18_ = bf16[2,3,3,16,1024]{4,3,2,1,0:T(8,128)(2,1)S(1)} collective-permute-done((bf16[2,3,3,16,1024]{4,3,2,1,0:T(8,128)(2,1)S(1)}, bf16[2,3,3,16,1024]{4,3,2,1,0:T(8,128)(2,1)S(1)}, u32[]{:S(2)}, u32[]{:S(2)}) %collective-permute-start.7) | collective-permute-done | bytes 589856 | tf_op jit(solution)/shard_map/ppermute | solution.py:355
  60.1 2.8 collective-permute-start.9
  69.1 12.0 %enter.1 = (bf16[4,512,256]{2,1,0:T(8,128)(2,1)}, bf16[4,512,256]{2,1,0:T(8,128)(2,1)S(1)}, bf16[4,2,512,256]{3,2,1,0:T(8,128)(2,1)S(1)}, bf16[4,3,528,256]{3,2,1,0:T(8,128)(2,1)}, bf16[512,1024]{1,0:T(8,128)(2,1)S(1)}) custom-call(s32[3]{0:T(128)S(1)} %pad_add_fusion.here_ref, f32[512,1024]{1,0:T(8,128)S(1)} %copy-done.7, ...), custom_call_target="tpu_custom_call" | custom-call | flops 3221225472 | bytes 16777216 | tf_op jit(solution)/shard_map/enter/pallas_call | solution.py:292
  84.4 5.4 %all-to-all-start = ((bf16[4,512,256]{2,1,0:T(8,128)(2,1)}), bf16[4,512,256]{2,1,0:T(8,128)(2,1)S(1)}, u32[]{:S(2)}, u32[]{:S(2)}) async-start(bf16[4,512,256]{2,1,0:T(8,128)(2,1)} %get-tuple-element.88.refs_1_), calls=%async_computation | async-start | bytes 2097152 | tf_op jit(solution)/shard_map/all_to_all | solution.py:1148
  96.4 8.6 %filter_taps.1 = (bf16[2048,256]{1,0:T(8,128)(2,1)S(1)}, f32[3,64,2048]{2,1,0:T(8,128)S(1)}, f32[3,64,2048]{2,1,0:T(8,128)S(1)}, f32[3,64,2048]{2,1,0:T(8,128)S(1)}) custom-call(s32[3]{0:T(128)S(1)} %pad_add_fusion.here_ref, f32[40,2048]{1,0:T(8,128)S(1)} %copy-done.24, f32[40,64]{1,0:T(8,128)S(1)} %pad.9.enter_ref, f32[64,64]{1,0:T(8,128)S(1)} %copy-done.11, ...), custom_call_target="tpu_custom_call" | custom-call | flops 4000000000 | bytes 6291456 | tf_op jit(solution)/shard_map/filter_taps/pallas_call | solution.py:292
  109.5 5.9 %all-to-all-done = bf16[4,512,256]{2,1,0:T(8,128)(2,1)S(1)} async-done(((bf16[4,512,256]{2,1,0:T(8,128)(2,1)}), bf16[4,512,256]{2,1,0:T(8,128)(2,1)S(1)}, u32[]{:S(2)}, u32[]{:S(2)}) %all-to-all-start) | async-done | bytes 1048608 | tf_op jit(solution)/shard_map/all_to_all | solution.py:1148
  115.4 2.7 pad_maximum_fusion.6.refs_11_
  118.9 3.0 pad_maximum_fusion.7.refs_15_
  122.6 13.9 %long_conv.1 = (bf16[32,64,256]{2,1,0:T(8,128)(2,1)}, bf16[64,64,256]{2,1,0:T(8,128)(2,1)S(1)}, bf16[64,64,256]{2,1,0:T(8,128)(2,1)S(1)}) custom-call(bf16[1024,512]{1,0:T(8,128)(2,1)S(1)} %copy-done.20, bf16[32,128,128]{2,1,0:T(8,128)(2,1)S(1)} %copy-done.18, bf16[32,128,128]{2,1,0:T(8,128)(2,1)S(1)} %copy-done.16, bf16[512,1024]{1,0:T(8,128)(2,1)S(1)} %copy-done.15, ...), custom_call_target="tpu_custom_call" | custom-call | flops 8999999488 | bytes 14680064 | tf_op jit(solution)/shard_map/long_conv/pallas_call | solution.py:292
  139.2 4.4 all-to-all-start.1
  144.4 3.2 collective-permute-start.16
  147.6 2.5 collective-permute-start.18
  150.2 10.2 %collective-permute-done.16.refs_2_ = bf16[4,2,16,256]{3,2,1,0:T(8,128)(2,1)S(1)} collective-permute-done((bf16[4,2,16,256]{3,2,1,0:T(8,128)(2,1)S(1)}, bf16[4,2,16,256]{3,2,1,0:T(8,128)(2,1)S(1)}, u32[]{:S(2)}, u32[]{:S(2)}) %collective-permute-start.16) | collective-permute-done | bytes 65568 | tf_op jit(solution)/shard_map/ppermute | solution.py:350
  160.4 8.5 %all-to-all-done.1.refs_0_ = bf16[4,512,256]{2,1,0:T(8,128)(2,1)} async-done(((bf16[4,512,256]{2,1,0:T(8,128)(2,1)}), bf16[4,512,256]{2,1,0:T(8,128)(2,1)}, u32[]{:S(2)}, u32[]{:S(2)}) %all-to-all-start.1) | async-done | bytes 1048608 | tf_op jit(solution)/shard_map/all_to_all | solution.py:1148
  168.9 2.2 collective-permute-start.19
  174.7 2.5 collective-permute-done.22.refs_18_
  177.2 44.5 %middle.1 = (f32[512,1024]{1,0:T(8,128)}, f32[512,1024]{1,0:T(8,128)}, bf16[4,512,256]{2,1,0:T(8,128)(2,1)}, bf16[4,512,256]{2,1,0:T(8,128)(2,1)}, bf16[512,1024...) custom-call(s32[3]{0:T(128)} %copy-done.5, ...), custom_call_target="tpu_custom_call" | custom-call | flops 20000000000 | bytes 50331648 | tf_op jit(solution)/shard_map/middle/pallas_call | solution.py:292
  221.7 3.5 all-to-all-start.2
  226.1 3.3 collective-permute-start.23
  229.4 6.3 %convolution_convert_fusion.1 = bf16[2048,1024]{1,0:T(8,128)(2,1)} fusion(bf16[512,1024]{1,0:T(8,128)(2,1)} %get-tuple-element.111, bf16[2,512,2048]{2,1,0:T(8,128)(2,1)} %get-tuple-element.110), kind=kOutput, calls=%fused_computation.7 | convolution fusion | flops 2149580800 | bytes 7340032 | tf_op jit(solution)/shard_map/dot_general | solution.py:446
  236.6 7.2 %collective-permute-done.23.refs_3_ = bf16[2,4,16,256]{3,2,1,0:T(8,128)(2,1)S(1)} collective-permute-done((bf16[2,4,16,256]{3,2,1,0:T(8,128)(2,1)S(1)}, bf16[2,4,16,256]{3,2,1,0:T(8,128)(2,1)S(1)}, u32[]{:S(2)}, u32[]{:S(2)}) %collective-permute-start.23) | collective-permute-done | bytes 65568 | tf_op jit(solution)/shard_map/ppermute | solution.py:350
  243.8 6.9 %all-to-all-done.2 = bf16[4,512,256]{2,1,0:T(8,128)(2,1)S(1)} async-done(((bf16[4,512,256]{2,1,0:T(8,128)(2,1)}), bf16[4,512,256]{2,1,0:T(8,128)(2,1)S(1)}, u32[]{:S(2)}, u32[]{:S(2)}) %all-to-all-start.2) | async-done | bytes 1048608 | tf_op jit(solution)/shard_map/all_to_all | solution.py:1148
  257.6 13.6 %long_conv_back.1 = (bf16[4,528,256]{2,1,0:T(8,128)(2,1)}, f32[32,64,256]{2,1,0:T(8,128)S(1)}) custom-call(bf16[1024,512]{1,0:T(8,128)(2,1)S(1)} %copy-done.21, bf16[32,128,128]{2,1,0:T(8,128)(2,1)S(1)} %copy-done.19, bf16[32,128,128]{2,1,0:T(8,128)(2,1)S(1)} %copy-done.17, bf16[512,1024]{1,0:T(8,128)(2,1)S(1)} %copy-done.15, ...), custom_call_target="tpu_custom_call" | custom-call | flops 8999999488 | bytes 14680064 | tf_op jit(solution)/shard_map/long_conv_back/pallas_call | solution.py:292
  271.2 4.4 convolution_convert_fusion
  275.6 1.9 collective-permute-start.25
  277.5 4.3 all-to-all-start.3
  282.0 5.2 %add_convert_fusion.2 = bf16[2048,1024]{1,0:T(8,128)(2,1)S(1)} fusion(bf16[2048,1024]{1,0:T(8,128)(2,1)} %collective-permute-done.24, bf16[512,1024]{1,0:T(8,128)(2,1)S(1)} %copy-done.61, bf16[2,512,2048]{2,1,0:T(8,128)(2,1)} %get-tuple-element.110), kind=kOutput, calls=%fused_computation.2 | convolution fusion | flops 2153775104 | bytes 11534336 | tf_op jit(solution)/shard_map/dot_general | solution.py:446
  289.7 4.6 add_convert_fusion.1
  294.3 1.8 slice_bitcast_fusion.2
  300.7 7.5 %all-to-all-done.3.refs_0_ = bf16[4,528,256]{2,1,0:T(8,128)(2,1)} async-done(((bf16[4,528,256]{2,1,0:T(8,128)(2,1)}), bf16[4,528,256]{2,1,0:T(8,128)(2,1)}, u32[]{:S(2)}, u32[]{:S(2)}) %all-to-all-start.3) | async-done | bytes 1081376 | tf_op jit(solution)/shard_map/all_to_all | solution.py:1148
  308.2 24.9 %leave.1 = (f32[512,1024]{1,0:T(8,128)}, f32[4,32,256]{2,1,0:T(8,128)}, f32[32,256]{1,0:T(8,128)}, bf16[2,2,2,8,32,1024]{5,4,3,2,1,0:T(8,128)(2,1)}, bf16[2,2,2,8,32,1024]{5,4,3,2,1,0:T(8,128)(2,1)}) custom-call(s32[3]{0:T(128)} %copy-done.5, bf16[4,528,256]{2,1,0:T(8,128)(2,1)} %all-to-all-done.3.refs_0_, bf16[4,512,256]{2,1,0:T(8,128)(2,1)} %get-tuple-element.102.refs_1_, ...), custom_call_target="tpu_custom_call" | custom-call | flops 16000000000 | bytes 35651584 | tf_op jit(solution)/shard_map/leave/pallas_call | solution.py:974
  335.9 9.1 %collective-permute-done.34 = bf16[2,2,2,128,1024]{4,3,2,1,0:T(8,128)(2,1)} collective-permute-done((bf16[2,2,2,128,1024]{4,3,2,1,0:T(8,128)(2,1)}, bf16[2,2,2,128,1024]{4,3,2,1,0:T(8,128)(2,1)}, u32[]{:S(2)}, u32[]{:S(2)}) %collective-permute-start.34) | collective-permute-done | bytes 2097184 | tf_op jit(solution)/shard_map/ppermute | solution.py:355
  345.0 2.6 fusion
  349.9 2.6 add_convert_fusion.3
  354.5 18.1 %collective-permute-done.35 = bf16[2,2,128,1024]{3,2,1,0:T(8,128)(2,1)S(1)} collective-permute-done((bf16[2,2,128,1024]{3,2,1,0:T(8,128)(2,1)}, bf16[2,2,128,1024]{3,2,1,0:T(8,128)(2,1)S(1)}, u32[]{:S(2)}, u32[]{:S(2)}) %collective-permute-start.35) | collective-permute-done | bytes 1048608 | tf_op jit(solution)/shard_map/ppermute | solution.py:355
  374.3 3.5 collective-permute-done.37
  380.8 5.6 %add_convert_fusion = bf16[2,2,2,8,32,1024]{5,4,3,2,1,0:T(8,128)(2,1)S(1)} fusion(bf16[2,2,2,8,32,1024]{5,4,3,2,1,0:T(8,128)(2,1)} %collective-permute-done.26, bf16[2,2,2,8,32,1024]{5,4,3,2,1,0:T(8,128)(2,1)} %get-tuple-element.127), kind=kLoop, calls=%fused_computation | loop fusion | flops 8388608 | bytes 12582912 | tf_op jit(solution)/shard_map/convert_element_type | solution.py:1247
  389.8 5.9 %filter_back.1 = (f32[64,256]{1,0:T(8,128)S(1)}, f32[64,256]{1,0:T(8,128)S(1)}) custom-call(s32[3]{0:T(128)S(1)} %copy-done.6, f32[40,2048]{1,0:T(8,128)S(1)} %copy-done.24, f32[64,64]{1,0:T(8,128)S(1)} %copy-done.11, f32[64,64]{1,0:T(8,128)S(1)} %copy-done.12, f32[64,4]{1,0:T(8,128)S(1)} %copy.90.columns_ref, f32[64,256]{1,0:T(8,128)S(1)} %copy-done.10, ...), custom_call_target="tpu_custom_call" | custom-call | flops 8000000000 | bytes 6291456 | tf_op jit(solution)/shard_map/filter_back/pallas_call | solution.py:292
  395.7 14.0 %collective-permute-done.28 = bf16[2,8,32,1024]{3,2,1,0:T(8,128)(2,1)S(1)} collective-permute-done((bf16[2,8,32,1024]{3,2,1,0:T(8,128)(2,1)S(1)}, bf16[2,8,32,1024]{3,2,1,0:T(8,128)(2,1)S(1)}, u32[]{:S(2)}, u32[]{:S(2)}) %collective-permute-start.28) | collective-permute-done | bytes 1048608 | tf_op jit(solution)/shard_map/ppermute | solution.py:355
  411.9 8.9 %collective-permute-done.33 = bf16[8,32,1024]{2,1,0:T(8,128)(2,1)S(1)} collective-permute-done((bf16[8,32,1024]{2,1,0:T(8,128)(2,1)S(1)}, bf16[8,32,1024]{2,1,0:T(8,128)(2,1)S(1)}, u32[]{:S(2)}, u32[]{:S(2)}) %collective-permute-start.33) | collective-permute-done | bytes 524320 | tf_op jit(solution)/shard_map/ppermute | solution.py:355
  423.1 2.3 reduce-scatter.5.cloned.1.call-done
  429.0 3.5 collective-permute-done.38
  432.5 1.8 collective-permute-start.39
  434.3 1.8 collective-permute-start.43
  436.2 2.4 collective-permute-start.29
  440.9 4.0 collective-permute-done.39.refs_1_
  444.9 5.3 %collective-permute-start.41 = (bf16[2,128,1024]{2,1,0:T(8,128)(2,1)S(1)}, bf16[2,128,1024]{2,1,0:T(8,128)(2,1)S(1)}, u32[]{:S(2)}, u32[]{:S(2)}) collective-permute-start(bf16[2,128,1024]{2,1,0:T(8,128)(2,1)S(1)} %collective-permute-done.39.refs_1_), channel_id=1, source_target_pairs={{0,4},{4,0},{8,12},{12,8},{16,20},{20,16},{24,28},{28,24},{1,5},{5... | collective-permute-start | bytes 1572872 | tf_op jit(solution)/shard_map/ppermute | solution.py:355
  453.1 5.1 %collective-permute-done.31 = f32[320,256]{1,0:T(8,128)S(1)} collective-permute-done((f32[320,256]{1,0:T(8,128)S(1)}, f32[320,256]{1,0:T(8,128)S(1)}, u32[]{:S(2)}, u32[]{:S(2)}) %collective-permute-start.31) | collective-permute-done | bytes 327712 | tf_op jit(solution)/shard_map/ppermute | solution.py:355
  458.9 4.7 place_feed.1
  465.9 2.3 collective-permute-start.53
  468.3 2.3 collective-permute-start.47
  472.0 4.8 collective-permute-start.51
  476.8 3.0 collective-permute-start.55
  481.3 3.4 collective-permute-done.50.refs_1_
  484.7 3.4 collective-permute-start.52
  488.0 4.6 collective-permute-start.56
  497.5 3.4 place_input.1
  (303 shorter events, 98.0 us)
Async XLA Ops:
  7.2 83.7 %all-gather.3.cloned.1.call-start = ((), (), s32[]{:S(2)}) async-start(), calls=%async_computation.8 | async-start | bytes 2949120 | tf_op jit(solution)/shard_map/all_gather | solution.py:1131
  10.4 16.0 %collective-permute-start.1 = (f32[96,256]{1,0:T(8,128)S(1)}, f32[96,256]{1,0:T(8,128)S(1)}, u32[]{:S(2)}, u32[]{:S(2)}) collective-permute-start(f32[96,256]{1,0:T(8,128)S(1)} %get-tuple-element.205), channel_id=1, source_target_pairs={{0,2},{1,3},{2,0},{3,1},{4,6},{5,7},{6,4},{7,5},{8,10},{9,11},{10,... | collective-permute-start | bytes 294920 | tf_op jit(solution)/shard_map/ppermute | solution.py:350
  13.6 14.1 %collective-permute-start.2 = (f32[96,256]{1,0:T(8,128)S(1)}, f32[96,256]{1,0:T(8,128)S(1)}, u32[]{:S(2)}, u32[]{:S(2)}) collective-permute-start(f32[96,256]{1,0:T(8,128)S(1)} %get-tuple-element.205), channel_id=1, source_target_pairs={{0,3},{1,0},{2,1},{3,2},{4,7},{5,4},{6,5},{7,6},{8,11},{9,8},{10,9... | collective-permute-start | bytes 294920 | tf_op jit(solution)/shard_map/ppermute | solution.py:350
  14.7 13.0 %collective-permute-start = (f32[96,256]{1,0:T(8,128)S(1)}, f32[96,256]{1,0:T(8,128)S(1)}, u32[]{:S(2)}, u32[]{:S(2)}) collective-permute-start(f32[96,256]{1,0:T(8,128)S(1)} %get-tuple-element.205), channel_id=1, source_target_pairs={{0,1},{1,2},{2,3},{3,0},{4,5},{5,6},{6,7},{7,4},{8,9},{9,10},{10,1... | collective-permute-start | bytes 294920 | tf_op jit(solution)/shard_map/ppermute | solution.py:350
  16.8 11.7 %collective-permute-start.5 = (bf16[3,32,1024]{2,1,0:T(8,128)(2,1)S(1)}, bf16[3,32,1024]{2,1,0:T(8,128)(2,1)S(1)}, u32[]{:S(2)}, u32[]{:S(2)}) collective-permute-start(bf16[3,32,1024]{2,1,0:T(8,128)(2,1)S(1)} %dynamic-slice_bitcast_fusion.1), channel_id=1, source_target_pairs={{0,3},{1,0},{2,1},{3,2},{4,7},{5,4},{6,5},{7,6},{8,11},{9,8},{10,9... | collective-permute-start | bytes 589832 | tf_op jit(solution)/shard_map/ppermute | solution.py:350
  19.8 19.6 %collective-permute-start.4 = (bf16[3,32,1024]{2,1,0:T(8,128)(2,1)S(1)}, bf16[3,32,1024]{2,1,0:T(8,128)(2,1)S(1)}, u32[]{:S(2)}, u32[]{:S(2)}) collective-permute-start(bf16[3,32,1024]{2,1,0:T(8,128)(2,1)S(1)} %dynamic-slice_bitcast_fusion.1), channel_id=1, source_target_pairs={{0,2},{1,3},{2,0},{3,1},{4,6},{5,7},{6,4},{7,5},{8,10},{9,11},{10,... | collective-permute-start | bytes 589832 | tf_op jit(solution)/shard_map/ppermute | solution.py:350
  26.4 12.9 %collective-permute-start.3 = (bf16[3,32,1024]{2,1,0:T(8,128)(2,1)S(1)}, bf16[3,32,1024]{2,1,0:T(8,128)(2,1)S(1)}, u32[]{:S(2)}, u32[]{:S(2)}) collective-permute-start(bf16[3,32,1024]{2,1,0:T(8,128)(2,1)S(1)} %dynamic-slice_bitcast_fusion.1), channel_id=1, source_target_pairs={{0,1},{1,2},{2,3},{3,0},{4,5},{5,6},{6,7},{7,4},{8,9},{9,10},{10,1... | collective-permute-start | bytes 589832 | tf_op jit(solution)/shard_map/ppermute | solution.py:350
  39.6 7.3 %collective-permute-start.6 = (bf16[3,3,16,1024]{3,2,1,0:T(8,128)(2,1)S(1)}, bf16[3,3,16,1024]{3,2,1,0:T(8,128)(2,1)S(1)}, u32[]{:S(2)}, u32[]{:S(2)}) collective-permute-start(bf16[3,3,16,1024]{3,2,1,0:T(8,128)(2,1)S(1)} %get-tuple-element.181), channel_id=1, source_target_pairs={{0,16},{4,20},{8,24},{12,28},{16,0},{20,4},{24,8},{28,12},{1,17},{... | collective-permute-start | bytes 884744 | tf_op jit(solution)/shard_map/ppermute | solution.py:355
  40.9 7.3 %collective-permute-start.10 = (bf16[3,3,16,1024]{3,2,1,0:T(8,128)(2,1)S(1)}, bf16[3,3,16,1024]{3,2,1,0:T(8,128)(2,1)S(1)}, u32[]{:S(2)}, u32[]{:S(2)}) collective-permute-start(bf16[3,3,16,1024]{3,2,1,0:T(8,128)(2,1)S(1)} %get-tuple-element.180), channel_id=1, source_target_pairs={{0,8},{4,12},{8,0},{12,4},{16,24},{20,28},{24,16},{28,20},{1,9},{5... | collective-permute-start | bytes 884744 | tf_op jit(solution)/shard_map/ppermute | solution.py:355
  47.0 13.1 %collective-permute-start.7 = (bf16[2,3,3,16,1024]{4,3,2,1,0:T(8,128)(2,1)S(1)}, bf16[2,3,3,16,1024]{4,3,2,1,0:T(8,128)(2,1)S(1)}, u32[]{:S(2)}, u32[]{:S(2)}) collective-permute-start(bf16[2,3,3,16,1024]{4,3,2,1,0:T(8,128)(2,1)S(1)} %pad_maximum_fusion.11.refs_0_.refs_17_), channel_id=1, source_target_pairs={{0,8},{4,12},{8,0},{12,4},{16,24},{20,28},{24,16},{28,20},{1,9},{5... | collective-permute-start | bytes 1769480 | tf_op jit(solution)/shard_map/ppermute | solution.py:355
  48.3 14.7 %collective-permute-start.11 = (bf16[2,3,3,16,1024]{4,3,2,1,0:T(8,128)(2,1)S(1)}, bf16[2,3,3,16,1024]{4,3,2,1,0:T(8,128)(2,1)}, u32[]{:S(2)}, u32[]{:S(2)}) collective-permute-start(bf16[2,3,3,16,1024]{4,3,2,1,0:T(8,128)(2,1)S(1)} %pad_maximum_fusion.12.refs_4_.refs_21_), channel_id=1, source_target_pairs={{0,16},{4,20},{8,24},{12,28},{16,0},{20,4},{24,8},{28,12},{1,17},{... | collective-permute-start | bytes 1769480 | tf_op jit(solution)/shard_map/ppermute | solution.py:355
  49.6 17.9 %collective-permute-start.8 = (bf16[2,3,3,16,1024]{4,3,2,1,0:T(8,128)(2,1)S(1)}, bf16[2,3,3,16,1024]{4,3,2,1,0:T(8,128)(2,1)}, u32[]{:S(2)}, u32[]{:S(2)}) collective-permute-start(bf16[2,3,3,16,1024]{4,3,2,1,0:T(8,128)(2,1)S(1)} %pad_maximum_fusion.11.refs_0_.refs_17_), channel_id=1, source_target_pairs={{0,4},{4,0},{8,12},{12,8},{16,20},{20,16},{24,28},{28,24},{1,5},{5... | collective-permute-start | bytes 1769480 | tf_op jit(solution)/shard_map/ppermute | solution.py:355
  52.4 15.1 %collective-permute-start.12 = (bf16[2,3,3,16,1024]{4,3,2,1,0:T(8,128)(2,1)S(1)}, bf16[2,3,3,16,1024]{4,3,2,1,0:T(8,128)(2,1)}, u32[]{:S(2)}, u32[]{:S(2)}) collective-permute-start(bf16[2,3,3,16,1024]{4,3,2,1,0:T(8,128)(2,1)S(1)} %pad_maximum_fusion.12.refs_4_.refs_21_), channel_id=1, source_target_pairs={{0,4},{4,0},{8,12},{12,8},{16,20},{20,16},{24,28},{28,24},{1,5},{5... | collective-permute-start | bytes 1769480 | tf_op jit(solution)/shard_map/ppermute | solution.py:355
  60.1 7.4 %collective-permute-start.9 = (bf16[2,3,3,16,1024]{4,3,2,1,0:T(8,128)(2,1)S(1)}, bf16[2,3,3,16,1024]{4,3,2,1,0:T(8,128)(2,1)}, u32[]{:S(2)}, u32[]{:S(2)}) collective-permute-start(bf16[2,3,3,16,1024]{4,3,2,1,0:T(8,128)(2,1)S(1)} %collective-permute-done.7.refs_1_.refs_18_), channel_id=1, source_target_pairs={{0,4},{4,0},{8,12},{12,8},{16,20},{20,16},{24,28},{28,24},{1,5},{5... | collective-permute-start | bytes 1769480 | tf_op jit(solution)/shard_map/ppermute | solution.py:355
  63.0 4.5 collective-permute-start.13
  84.4 31.0 %all-to-all-start = ((bf16[4,512,256]{2,1,0:T(8,128)(2,1)}), bf16[4,512,256]{2,1,0:T(8,128)(2,1)S(1)}, u32[]{:S(2)}, u32[]{:S(2)}) async-start(bf16[4,512,256]{2,1,0:T(8,128)(2,1)} %get-tuple-element.88.refs_1_), calls=%async_computation | async-start | bytes 2097152 | tf_op jit(solution)/shard_map/all_to_all | solution.py:1148
  93.8 21.6 %collective-permute-start.14 = (bf16[3,144,1024]{2,1,0:T(8,128)(2,1)S(1)}, bf16[3,144,1024]{2,1,0:T(8,128)(2,1)}, u32[]{:S(2)}, u32[]{:S(2)}) collective-permute-start(bf16[3,144,1024]{2,1,0:T(8,128)(2,1)S(1)} %get-tuple-element.91), channel_id=1, source_target_pairs={{0,16},{4,20},{8,24},{12,28},{16,0},{20,4},{24,8},{28,12},{1,17},{... | collective-permute-start | bytes 2654216 | tf_op jit(solution)/shard_map/ppermute | solution.py:355
  95.0 23.9 %collective-permute-start.15 = (bf16[3,144,1024]{2,1,0:T(8,128)(2,1)}, bf16[3,144,1024]{2,1,0:T(8,128)(2,1)}, u32[]{:S(2)}, u32[]{:S(2)}) collective-permute-start(bf16[3,144,1024]{2,1,0:T(8,128)(2,1)} %get-tuple-element.92), channel_id=1, source_target_pairs={{0,8},{4,12},{8,0},{12,4},{16,24},{20,28},{24,16},{28,20},{1,9},{5... | collective-permute-start | bytes 2654216 | tf_op jit(solution)/shard_map/ppermute | solution.py:355
  118.2 50.7 %collective-permute-start.17 = (bf16[2,3,144,1024]{3,2,1,0:T(8,128)(2,1)}, bf16[2,3,144,1024]{3,2,1,0:T(8,128)(2,1)}, u32[]{:S(2)}, u32[]{:S(2)}) collective-permute-start(bf16[2,3,144,1024]{3,2,1,0:T(8,128)(2,1)} %pad_maximum_fusion.6.refs_11_), channel_id=1, source_target_pairs={{0,8},{4,12},{8,0},{12,4},{16,24},{20,28},{24,16},{28,20},{1,9},{5... | collective-permute-start | bytes 5308424 | tf_op jit(solution)/shard_map/ppermute | solution.py:355
  121.9 47.0 %collective-permute-start.20 = (bf16[2,3,144,1024]{3,2,1,0:T(8,128)(2,1)}, bf16[2,3,144,1024]{3,2,1,0:T(8,128)(2,1)}, u32[]{:S(2)}, u32[]{:S(2)}) collective-permute-start(bf16[2,3,144,1024]{3,2,1,0:T(8,128)(2,1)} %pad_maximum_fusion.7.refs_15_), channel_id=1, source_target_pairs={{0,16},{4,20},{8,24},{12,28},{16,0},{20,4},{24,8},{28,12},{1,17},{... | collective-permute-start | bytes 5308424 | tf_op jit(solution)/shard_map/ppermute | solution.py:355
  139.2 29.7 %all-to-all-start.1 = ((bf16[4,512,256]{2,1,0:T(8,128)(2,1)}), bf16[4,512,256]{2,1,0:T(8,128)(2,1)}, u32[]{:S(2)}, u32[]{:S(2)}) async-start(bf16[4,512,256]{2,1,0:T(8,128)(2,1)} %bitcast.34), calls=%async_computation.1 | async-start | bytes 2097152 | tf_op jit(solution)/shard_map/all_to_all | solution.py:1148
  144.4 15.9 %collective-permute-start.16 = (bf16[4,2,16,256]{3,2,1,0:T(8,128)(2,1)S(1)}, bf16[4,2,16,256]{3,2,1,0:T(8,128)(2,1)S(1)}, u32[]{:S(2)}, u32[]{:S(2)}) collective-permute-start(bf16[4,2,16,256]{3,2,1,0:T(8,128)(2,1)S(1)} %slice.258), channel_id=1, source_target_pairs={{0,3},{1,0},{2,1},{3,2},{4,7},{5,4},{6,5},{7,6},{8,11},{9,8},{10,9... | collective-permute-start | bytes 196616 | tf_op jit(solution)/shard_map/ppermute | solution.py:350
  147.6 25.5 %collective-permute-start.18 = (bf16[2,3,144,1024]{3,2,1,0:T(8,128)(2,1)}, bf16[2,3,144,1024]{3,2,1,0:T(8,128)(2,1)}, u32[]{:S(2)}, u32[]{:S(2)}) collective-permute-start(bf16[2,3,144,1024]{3,2,1,0:T(8,128)(2,1)} %pad_maximum_fusion.6.refs_11_), channel_id=1, source_target_pairs={{0,4},{4,0},{8,12},{12,8},{16,20},{20,16},{24,28},{28,24},{1,5},{5... | collective-permute-start | bytes 5308424 | tf_op jit(solution)/shard_map/ppermute | solution.py:355
  150.2 23.0 %collective-permute-start.21 = (bf16[2,3,144,1024]{3,2,1,0:T(8,128)(2,1)}, bf16[2,3,144,1024]{3,2,1,0:T(8,128)(2,1)}, u32[]{:S(2)}, u32[]{:S(2)}) collective-permute-start(bf16[2,3,144,1024]{3,2,1,0:T(8,128)(2,1)} %pad_maximum_fusion.7.refs_15_), channel_id=1, source_target_pairs={{0,4},{4,0},{8,12},{12,8},{16,20},{20,16},{24,28},{28,24},{1,5},{5... | collective-permute-start | bytes 5308424 | tf_op jit(solution)/shard_map/ppermute | solution.py:355
  168.9 5.8 %collective-permute-start.19 = (bf16[2,3,144,1024]{3,2,1,0:T(8,128)(2,1)}, bf16[2,3,144,1024]{3,2,1,0:T(8,128)(2,1)}, u32[]{:S(2)}, u32[]{:S(2)}) collective-permute-start(bf16[2,3,144,1024]{3,2,1,0:T(8,128)(2,1)} %collective-permute-done.17.refs_12_), channel_id=1, source_target_pairs={{0,4},{4,0},{8,12},{12,8},{16,20},{20,16},{24,28},{28,24},{1,5},{5... | collective-permute-start | bytes 5308424 | tf_op jit(solution)/shard_map/ppermute | solution.py:355
  171.0 6.2 %collective-permute-start.22 = (bf16[2,3,144,1024]{3,2,1,0:T(8,128)(2,1)}, bf16[2,3,144,1024]{3,2,1,0:T(8,128)(2,1)}, u32[]{:S(2)}, u32[]{:S(2)}) collective-permute-start(bf16[2,3,144,1024]{3,2,1,0:T(8,128)(2,1)} %collective-permute-done.20.refs_16_), channel_id=1, source_target_pairs={{0,4},{4,0},{8,12},{12,8},{16,20},{20,16},{24,28},{28,24},{1,5},{5... | collective-permute-start | bytes 5308424 | tf_op jit(solution)/shard_map/ppermute | solution.py:355
  221.7 29.0 %all-to-all-start.2 = ((bf16[4,512,256]{2,1,0:T(8,128)(2,1)}), bf16[4,512,256]{2,1,0:T(8,128)(2,1)S(1)}, u32[]{:S(2)}, u32[]{:S(2)}) async-start(bf16[4,512,256]{2,1,0:T(8,128)(2,1)} %get-tuple-element.102.refs_1_), calls=%async_computation.2 | async-start | bytes 2097152 | tf_op jit(solution)/shard_map/all_to_all | solution.py:1148
  226.1 17.7 %collective-permute-start.23 = (bf16[2,4,16,256]{3,2,1,0:T(8,128)(2,1)S(1)}, bf16[2,4,16,256]{3,2,1,0:T(8,128)(2,1)S(1)}, u32[]{:S(2)}, u32[]{:S(2)}) collective-permute-start(bf16[2,4,16,256]{3,2,1,0:T(8,128)(2,1)S(1)} %pad_maximum_fusion.24), channel_id=1, source_target_pairs={{0,3},{1,0},{2,1},{3,2},{4,7},{5,4},{6,5},{7,6},{8,11},{9,8},{10,9... | collective-permute-start | bytes 196616 | tf_op jit(solution)/shard_map/ppermute | solution.py:350
  235.6 46.3 %collective-permute-start.24 = (bf16[2048,1024]{1,0:T(8,128)(2,1)}, bf16[2048,1024]{1,0:T(8,128)(2,1)}, u32[]{:S(2)}, u32[]{:S(2)}) collective-permute-start(bf16[2048,1024]{1,0:T(8,128)(2,1)} %convolution_convert_fusion.1), channel_id=1, source_target_pairs={{0,4},{4,0},{8,12},{12,8},{16,20},{20,16},{24,28},{28,24},{1,5},{5... | collective-permute-start | bytes 12582920 | tf_op jit(solution)/shard_map/ppermute | solution.py:355
  275.6 12.1 %collective-permute-start.25 = (bf16[2048,1024]{1,0:T(8,128)(2,1)}, bf16[2048,1024]{1,0:T(8,128)(2,1)}, u32[]{:S(2)}, u32[]{:S(2)}) collective-permute-start(bf16[2048,1024]{1,0:T(8,128)(2,1)} %convolution_convert_fusion), channel_id=1, source_target_pairs={{0,4},{4,0},{8,12},{12,8},{16,20},{20,16},{24,28},{28,24},{1,5},{5... | collective-permute-start | bytes 12582920 | tf_op jit(solution)/shard_map/ppermute | solution.py:355
  277.5 30.7 %all-to-all-start.3 = ((bf16[4,528,256]{2,1,0:T(8,128)(2,1)}), bf16[4,528,256]{2,1,0:T(8,128)(2,1)}, u32[]{:S(2)}, u32[]{:S(2)}) async-start(bf16[4,528,256]{2,1,0:T(8,128)(2,1)} %get-tuple-element.107), calls=%async_computation.3 | async-start | bytes 2162688 | tf_op jit(solution)/shard_map/all_to_all | solution.py:1148
  281.7 143.6 %reduce-scatter.5.cloned.1.call-start = ((), (), s32[]{:S(2)}) async-start(), calls=%async_computation.7 | async-start | bytes 2621440 | tf_op jit(solution)/shard_map/reduce_scatter | solution.py:1288
  297.6 47.4 %collective-permute-start.34 = (bf16[2,2,2,128,1024]{4,3,2,1,0:T(8,128)(2,1)}, bf16[2,2,2,128,1024]{4,3,2,1,0:T(8,128)(2,1)}, u32[]{:S(2)}, u32[]{:S(2)}) collective-permute-start(bf16[2,2,2,128,1024]{4,3,2,1,0:T(8,128)(2,1)} %pad_maximum_fusion), channel_id=1, source_target_pairs={{0,16},{4,20},{8,24},{12,28},{16,0},{20,4},{24,8},{28,12},{1,17},{... | collective-permute-start | bytes 6291464 | tf_op jit(solution)/shard_map/ppermute | solution.py:355
  300.0 49.9 %collective-permute-start.36 = (bf16[2,2,2,128,1024]{4,3,2,0,1:T(8,128)(2,1)}, bf16[2,2,2,128,1024]{4,3,2,0,1:T(8,128)(2,1)}, u32[]{:S(2)}, u32[]{:S(2)}) collective-permute-start(bf16[2,2,2,128,1024]{4,3,2,0,1:T(8,128)(2,1)} %pad_maximum_fusion.1), channel_id=1, source_target_pairs={{0,8},{4,12},{8,0},{12,4},{16,24},{20,28},{24,16},{28,20},{1,9},{5... | collective-permute-start | bytes 6291464 | tf_op jit(solution)/shard_map/ppermute | solution.py:355
  333.2 47.6 %collective-permute-start.26 = (bf16[2,2,2,8,32,1024]{5,4,3,2,1,0:T(8,128)(2,1)}, bf16[2,2,2,8,32,1024]{5,4,3,2,1,0:T(8,128)(2,1)}, u32[]{:S(2)}, u32[]{:S(2)}) collective-permute-start(bf16[2,2,2,8,32,1024]{5,4,3,2,1,0:T(8,128)(2,1)} %get-tuple-element.128), channel_id=1, source_target_pairs={{0,4},{4,0},{8,12},{12,8},{16,20},{20,16},{24,28},{28,24},{1,5},{5... | collective-permute-start | bytes 12582920 | tf_op jit(solution)/shard_map/ppermute | solution.py:355
  348.7 23.9 %collective-permute-start.35 = (bf16[2,2,128,1024]{3,2,1,0:T(8,128)(2,1)}, bf16[2,2,128,1024]{3,2,1,0:T(8,128)(2,1)S(1)}, u32[]{:S(2)}, u32[]{:S(2)}) collective-permute-start(bf16[2,2,128,1024]{3,2,1,0:T(8,128)(2,1)} %slice_bitcast_fusion.4), channel_id=1, source_target_pairs={{0,8},{4,12},{8,0},{12,4},{16,24},{20,28},{24,16},{28,20},{1,9},{5... | collective-permute-start | bytes 3145736 | tf_op jit(solution)/shard_map/ppermute | solution.py:355
  354.1 23.6 %collective-permute-start.37 = (bf16[2,2,128,1024]{3,2,1,0:T(8,128)(2,1)}, bf16[2,2,128,1024]{3,2,1,0:T(8,128)(2,1)S(1)}, u32[]{:S(2)}, u32[]{:S(2)}) collective-permute-start(bf16[2,2,128,1024]{3,2,1,0:T(8,128)(2,1)} %slice_bitcast_fusion), channel_id=1, source_target_pairs={{0,16},{4,20},{8,24},{12,28},{16,0},{20,4},{24,8},{28,12},{1,17},{... | collective-permute-start | bytes 3145736 | tf_op jit(solution)/shard_map/ppermute | solution.py:355
  380.5 83.1 %reduce-scatter.3.cloned.1.call-start = ((), (), s32[]{:S(2)}) async-start(), calls=%async_computation.6 | async-start | bytes 1310720 | tf_op jit(solution)/shard_map/reduce_scatter | solution.py:1295
  387.1 22.7 %collective-permute-start.28 = (bf16[2,8,32,1024]{3,2,1,0:T(8,128)(2,1)S(1)}, bf16[2,8,32,1024]{3,2,1,0:T(8,128)(2,1)S(1)}, u32[]{:S(2)}, u32[]{:S(2)}) collective-permute-start(bf16[2,8,32,1024]{3,2,1,0:T(8,128)(2,1)S(1)} %get-tuple-element.162), channel_id=1, source_target_pairs={{0,8},{4,12},{8,0},{12,4},{16,24},{20,28},{24,16},{28,20},{1,9},{5... | collective-permute-start | bytes 3145736 | tf_op jit(solution)/shard_map/ppermute | solution.py:355
  387.5 23.2 %collective-permute-start.27 = (bf16[2,8,32,1024]{3,2,1,0:T(8,128)(2,1)S(1)}, bf16[2,8,32,1024]{3,2,1,0:T(8,128)(2,1)S(1)}, u32[]{:S(2)}, u32[]{:S(2)}) collective-permute-start(bf16[2,8,32,1024]{3,2,1,0:T(8,128)(2,1)S(1)} %get-tuple-element.163), channel_id=1, source_target_pairs={{0,16},{4,20},{8,24},{12,28},{16,0},{20,4},{24,8},{28,12},{1,17},{... | collective-permute-start | bytes 3145736 | tf_op jit(solution)/shard_map/ppermute | solution.py:355
  410.2 10.6 %collective-permute-start.33 = (bf16[8,32,1024]{2,1,0:T(8,128)(2,1)S(1)}, bf16[8,32,1024]{2,1,0:T(8,128)(2,1)S(1)}, u32[]{:S(2)}, u32[]{:S(2)}) collective-permute-start(bf16[8,32,1024]{2,1,0:T(8,128)(2,1)S(1)} %slice_bitcast_fusion.16), channel_id=1, source_target_pairs={{0,16},{4,20},{8,24},{12,28},{16,0},{20,4},{24,8},{28,12},{1,17},{... | collective-permute-start | bytes 1572872 | tf_op jit(solution)/shard_map/ppermute | solution.py:355
  411.2 10.3 %collective-permute-start.32 = (bf16[8,32,1024]{2,1,0:T(8,128)(2,1)S(1)}, bf16[8,32,1024]{2,1,0:T(8,128)(2,1)S(1)}, u32[]{:S(2)}, u32[]{:S(2)}) collective-permute-start(bf16[8,32,1024]{2,1,0:T(8,128)(2,1)S(1)} %slice_bitcast_fusion.18), channel_id=1, source_target_pairs={{0,8},{4,12},{8,0},{12,4},{16,24},{20,28},{24,16},{28,20},{1,9},{5... | collective-permute-start | bytes 1572872 | tf_op jit(solution)/shard_map/ppermute | solution.py:355
  426.5 6.0 %collective-permute-start.38 = (bf16[128,1024]{1,0:T(8,128)(2,1)S(1)}, bf16[128,1024]{1,0:T(8,128)(2,1)S(1)}, u32[]{:S(2)}, u32[]{:S(2)}) collective-permute-start(bf16[128,1024]{1,0:T(8,128)(2,1)S(1)} %get-tuple-element.185), channel_id=1, source_target_pairs={{0,16},{4,20},{8,24},{12,28},{16,0},{20,4},{24,8},{28,12},{1,17},{... | collective-permute-start | bytes 786440 | tf_op jit(solution)/shard_map/ppermute | solution.py:355
  427.8 6.5 %collective-permute-start.42 = (bf16[128,1024]{1,0:T(8,128)(2,1)S(1)}, bf16[128,1024]{1,0:T(8,128)(2,1)S(1)}, u32[]{:S(2)}, u32[]{:S(2)}) collective-permute-start(bf16[128,1024]{1,0:T(8,128)(2,1)S(1)} %get-tuple-element.184), channel_id=1, source_target_pairs={{0,8},{4,12},{8,0},{12,4},{16,24},{20,28},{24,16},{28,20},{1,9},{5... | collective-permute-start | bytes 786440 | tf_op jit(solution)/shard_map/ppermute | solution.py:355
  432.5 12.4 %collective-permute-start.39 = (bf16[2,128,1024]{2,1,0:T(8,128)(2,1)S(1)}, bf16[2,128,1024]{2,1,0:T(8,128)(2,1)S(1)}, u32[]{:S(2)}, u32[]{:S(2)}) collective-permute-start(bf16[2,128,1024]{2,1,0:T(8,128)(2,1)S(1)} %pad_maximum_fusion.14.refs_0_), channel_id=1, source_target_pairs={{0,8},{4,12},{8,0},{12,4},{16,24},{20,28},{24,16},{28,20},{1,9},{5... | collective-permute-start | bytes 1572872 | tf_op jit(solution)/shard_map/ppermute | solution.py:355
  434.3 15.9 %collective-permute-start.43 = (bf16[2,128,1024]{2,1,0:T(8,128)(2,1)S(1)}, bf16[2,128,1024]{2,1,0:T(8,128)(2,1)S(1)}, u32[]{:S(2)}, u32[]{:S(2)}) collective-permute-start(bf16[2,128,1024]{2,1,0:T(8,128)(2,1)S(1)} %pad_maximum_fusion.15.refs_4_), channel_id=1, source_target_pairs={{0,16},{4,20},{8,24},{12,28},{16,0},{20,4},{24,8},{28,12},{1,17},{... | collective-permute-start | bytes 1572872 | tf_op jit(solution)/shard_map/ppermute | solution.py:355
  436.2 3.6 collective-permute-start.29
  439.8 12.0 %collective-permute-start.30 = (f32[320,256]{1,0:T(8,128)S(1)}, f32[320,256]{1,0:T(8,128)S(1)}, u32[]{:S(2)}, u32[]{:S(2)}) collective-permute-start(f32[320,256]{1,0:T(8,128)S(1)} %add.137), channel_id=1, source_target_pairs={{0,8},{4,12},{8,0},{12,4},{16,24},{20,28},{24,16},{28,20},{1,9},{5... | collective-permute-start | bytes 983048 | tf_op jit(solution)/shard_map/ppermute | solution.py:355
  440.2 18.7 %collective-permute-start.40 = (bf16[2,128,1024]{2,1,0:T(8,128)(2,1)S(1)}, bf16[2,128,1024]{2,1,0:T(8,128)(2,1)S(1)}, u32[]{:S(2)}, u32[]{:S(2)}) collective-permute-start(bf16[2,128,1024]{2,1,0:T(8,128)(2,1)S(1)} %pad_maximum_fusion.14.refs_0_), channel_id=1, source_target_pairs={{0,4},{4,0},{8,12},{12,8},{16,20},{20,16},{24,28},{28,24},{1,5},{5... | collective-permute-start | bytes 1572872 | tf_op jit(solution)/shard_map/ppermute | solution.py:355
  440.9 18.0 %collective-permute-start.44 = (bf16[2,128,1024]{2,1,0:T(8,128)(2,1)S(1)}, bf16[2,128,1024]{2,1,0:T(8,128)(2,1)S(1)}, u32[]{:S(2)}, u32[]{:S(2)}) collective-permute-start(bf16[2,128,1024]{2,1,0:T(8,128)(2,1)S(1)} %pad_maximum_fusion.15.refs_4_), channel_id=1, source_target_pairs={{0,4},{4,0},{8,12},{12,8},{16,20},{20,16},{24,28},{28,24},{1,5},{5... | collective-permute-start | bytes 1572872 | tf_op jit(solution)/shard_map/ppermute | solution.py:355
  444.9 14.0 %collective-permute-start.41 = (bf16[2,128,1024]{2,1,0:T(8,128)(2,1)S(1)}, bf16[2,128,1024]{2,1,0:T(8,128)(2,1)S(1)}, u32[]{:S(2)}, u32[]{:S(2)}) collective-permute-start(bf16[2,128,1024]{2,1,0:T(8,128)(2,1)S(1)} %collective-permute-done.39.refs_1_), channel_id=1, source_target_pairs={{0,4},{4,0},{8,12},{12,8},{16,20},{20,16},{24,28},{28,24},{1,5},{5... | collective-permute-start | bytes 1572872 | tf_op jit(solution)/shard_map/ppermute | solution.py:355
  450.3 8.7 %collective-permute-start.45 = (bf16[2,128,1024]{2,1,0:T(8,128)(2,1)S(1)}, bf16[2,128,1024]{2,1,0:T(8,128)(2,1)S(1)}, u32[]{:S(2)}, u32[]{:S(2)}) collective-permute-start(bf16[2,128,1024]{2,1,0:T(8,128)(2,1)S(1)} %collective-permute-done.43.refs_5_), channel_id=1, source_target_pairs={{0,4},{4,0},{8,12},{12,8},{16,20},{20,16},{24,28},{28,24},{1,5},{5... | collective-permute-start | bytes 1572872 | tf_op jit(solution)/shard_map/ppermute | solution.py:355
  451.9 6.3 %collective-permute-start.31 = (f32[320,256]{1,0:T(8,128)S(1)}, f32[320,256]{1,0:T(8,128)S(1)}, u32[]{:S(2)}, u32[]{:S(2)}) collective-permute-start(f32[320,256]{1,0:T(8,128)S(1)} %add.138), channel_id=1, source_target_pairs={{0,16},{4,20},{8,24},{12,28},{16,0},{20,4},{24,8},{28,12},{1,17},{... | collective-permute-start | bytes 983048 | tf_op jit(solution)/shard_map/ppermute | solution.py:355
  464.6 7.3 %collective-permute-start.49 = (bf16[4,16,1024]{2,1,0:T(8,128)(2,1)S(1)}, bf16[4,16,1024]{2,1,0:T(8,128)(2,1)S(1)}, u32[]{:S(2)}, u32[]{:S(2)}) collective-permute-start(bf16[4,16,1024]{2,1,0:T(8,128)(2,1)S(1)} %get-tuple-element.195), channel_id=1, source_target_pairs={{0,16},{4,20},{8,24},{12,28},{16,0},{20,4},{24,8},{28,12},{1,17},{... | collective-permute-start | bytes 393224 | tf_op jit(solution)/shard_map/ppermute | solution.py:355
  465.9 10.9 %collective-permute-start.53 = (bf16[4,16,1024]{2,1,0:T(8,128)(2,1)S(1)}, bf16[4,16,1024]{2,1,0:T(8,128)(2,1)S(1)}, u32[]{:S(2)}, u32[]{:S(2)}) collective-permute-start(bf16[4,16,1024]{2,1,0:T(8,128)(2,1)S(1)} %get-tuple-element.194), channel_id=1, source_target_pairs={{0,8},{4,12},{8,0},{12,4},{16,24},{20,28},{24,16},{28,20},{1,9},{5... | collective-permute-start | bytes 393224 | tf_op jit(solution)/shard_map/ppermute | solution.py:355
  468.2 8.6 %collective-permute-start.46 = (f32[160,256]{1,0:T(8,128)S(1)}, f32[160,256]{1,0:T(8,128)S(1)}, u32[]{:S(2)}, u32[]{:S(2)}) collective-permute-start(f32[160,256]{1,0:T(8,128)S(1)} %get-tuple-element.201), channel_id=1, source_target_pairs={{0,3},{1,0},{2,1},{3,2},{4,7},{5,4},{6,5},{7,6},{8,11},{9,8},{10,9... | collective-permute-start | bytes 491528 | tf_op jit(solution)/shard_map/ppermute | solution.py:350
  468.3 11.6 %collective-permute-start.47 = (f32[160,256]{1,0:T(8,128)S(1)}, f32[160,256]{1,0:T(8,128)S(1)}, u32[]{:S(2)}, u32[]{:S(2)}) collective-permute-start(f32[160,256]{1,0:T(8,128)S(1)} %get-tuple-element.202), channel_id=1, source_target_pairs={{0,2},{1,3},{2,0},{3,1},{4,6},{5,7},{6,4},{7,5},{8,10},{9,11},{10,... | collective-permute-start | bytes 491528 | tf_op jit(solution)/shard_map/ppermute | solution.py:350
  470.6 9.3 %collective-permute-start.48 = (f32[160,256]{1,0:T(8,128)S(1)}, f32[160,256]{1,0:T(8,128)S(1)}, u32[]{:S(2)}, u32[]{:S(2)}) collective-permute-start(f32[160,256]{1,0:T(8,128)S(1)} %get-tuple-element.203), channel_id=1, source_target_pairs={{0,1},{1,2},{2,3},{3,0},{4,5},{5,6},{6,7},{7,4},{8,9},{9,10},{10,1... | collective-permute-start | bytes 491528 | tf_op jit(solution)/shard_map/ppermute | solution.py:350
  472.0 25.5 %collective-permute-start.51 = (bf16[2,4,16,1024]{3,2,1,0:T(8,128)(2,1)S(1)}, bf16[2,4,16,1024]{3,2,1,0:T(8,128)(2,1)S(1)}, u32[]{:S(2)}, u32[]{:S(2)}) collective-permute-start(bf16[2,4,16,1024]{3,2,1,0:T(8,128)(2,1)S(1)} %pad_maximum_fusion.17.refs_0_), channel_id=1, source_target_pairs={{0,4},{4,0},{8,12},{12,8},{16,20},{20,16},{24,28},{28,24},{1,5},{5... | collective-permute-start | bytes 786440 | tf_op jit(solution)/shard_map/ppermute | solution.py:355
  476.8 7.9 %collective-permute-start.50 = (bf16[2,4,16,1024]{3,2,1,0:T(8,128)(2,1)S(1)}, bf16[2,4,16,1024]{3,2,1,0:T(8,128)(2,1)S(1)}, u32[]{:S(2)}, u32[]{:S(2)}) collective-permute-start(bf16[2,4,16,1024]{3,2,1,0:T(8,128)(2,1)S(1)} %pad_maximum_fusion.17.refs_0_), channel_id=1, source_target_pairs={{0,8},{4,12},{8,0},{12,4},{16,24},{20,28},{24,16},{28,20},{1,9},{5... | collective-permute-start | bytes 786440 | tf_op jit(solution)/shard_map/ppermute | solution.py:355
  476.8 20.7 %collective-permute-start.55 = (bf16[2,4,16,1024]{3,2,1,0:T(8,128)(2,1)S(1)}, bf16[2,4,16,1024]{3,2,1,0:T(8,128)(2,1)S(1)}, u32[]{:S(2)}, u32[]{:S(2)}) collective-permute-start(bf16[2,4,16,1024]{3,2,1,0:T(8,128)(2,1)S(1)} %pad_maximum_fusion.18.refs_4_), channel_id=1, source_target_pairs={{0,4},{4,0},{8,12},{12,8},{16,20},{20,16},{24,28},{28,24},{1,5},{5... | collective-permute-start | bytes 786440 | tf_op jit(solution)/shard_map/ppermute | solution.py:355
  479.9 8.1 %collective-permute-start.54 = (bf16[2,4,16,1024]{3,2,1,0:T(8,128)(2,1)S(1)}, bf16[2,4,16,1024]{3,2,1,0:T(8,128)(2,1)S(1)}, u32[]{:S(2)}, u32[]{:S(2)}) collective-permute-start(bf16[2,4,16,1024]{3,2,1,0:T(8,128)(2,1)S(1)} %pad_maximum_fusion.18.refs_4_), channel_id=1, source_target_pairs={{0,16},{4,20},{8,24},{12,28},{16,0},{20,4},{24,8},{28,12},{1,17},{... | collective-permute-start | bytes 786440 | tf_op jit(solution)/shard_map/ppermute | solution.py:355
  484.7 12.8 %collective-permute-start.52 = (bf16[2,4,16,1024]{3,2,1,0:T(8,128)(2,1)S(1)}, bf16[2,4,16,1024]{3,2,1,0:T(8,128)(2,1)S(1)}, u32[]{:S(2)}, u32[]{:S(2)}) collective-permute-start(bf16[2,4,16,1024]{3,2,1,0:T(8,128)(2,1)S(1)} %collective-permute-done.50.refs_1_), channel_id=1, source_target_pairs={{0,4},{4,0},{8,12},{12,8},{16,20},{20,16},{24,28},{28,24},{1,5},{5... | collective-permute-start | bytes 786440 | tf_op jit(solution)/shard_map/ppermute | solution.py:355
  488.0 9.5 %collective-permute-start.56 = (bf16[2,4,16,1024]{3,2,1,0:T(8,128)(2,1)S(1)}, bf16[2,4,16,1024]{3,2,1,0:T(8,128)(2,1)S(1)}, u32[]{:S(2)}, u32[]{:S(2)}) collective-permute-start(bf16[2,4,16,1024]{3,2,1,0:T(8,128)(2,1)S(1)} %collective-permute-done.54.refs_5_), channel_id=1, source_target_pairs={{0,4},{4,0},{8,12},{12,8},{16,20},{20,16},{24,28},{28,24},{1,5},{5... | collective-permute-start | bytes 786440 | tf_op jit(solution)/shard_map/ppermute | solution.py:355
  (62 other events, 659.5 us)
Sparse Core Ops, SparseCore 0:
  39.5 51.3 all-gather.2
  380.7 44.6 reduce-scatter.4
  428.3 26.4 reduce-scatter.2
